TPU v7x, 256 devices: a whole 4x4x8 slice. The times are simulated.
256 devices in a mesh: seq: 32 (over x, y, core), head: 8 (over z).
Axes of the slice: x: 4, y: 4, z: 8, core: 2. Of those that a mesh axis runs over, the one named last changes fastest.
Arguments:
- queries: bfloat16 [16384, 2048], P('seq', 'head'), may hold values from -6 to 6
- keys: bfloat16 [16384, 2048], P('seq', 'head'), may hold values from -6 to 6
- values: bfloat16 [16384, 2048], P('seq', 'head'), may hold values from -6 to 6
- attn_out: bfloat16 [16384, 2048], P('seq', 'head'), may hold values from -4 to 4
- out_grad: bfloat16 [16384, 4096], P(('seq', 'head')), may hold values from -48 to 48
- out_weight: bfloat16 [2048, 4096], P('head'), may hold values from -0.125 to 0.125
- log_norm: bfloat16 [16384, 16], P('seq', 'head'), may hold values from 0 to 13
- block_sizes: int32 [512], replicated, may hold values from 1 to 31, as said below
Outputs:
- query_grad: bfloat16 [16384, 2048], P('seq', 'head')
- key_grad: bfloat16 [16384, 2048], P('seq', 'head')
- value_grad: bfloat16 [16384, 2048], P('seq', 'head')
Inputs may be any that keep to these rules, and one draw needn't show every extreme that they name: `block_sizes`: blocks come in aligned pairs whose sizes add to 32; one block has exactly 31 tokens.
All inputs are finite; a program needn't handle non-finite values.
Results may differ from a plain program's by a relative error of at most 0.018.
Values may be sent and summed in bfloat16 or wider, within the bound.
A program may use at most 128 MiB of HBM per device.

v0:
```python
import jax
import jax.numpy as jnp
from jax import lax
from jax.sharding import PartitionSpec as P

HD = 128


def block_index(within, ends):
    return jnp.sum((within[:, None] >= ends[None, :]).astype(jnp.int32), axis=1)


def allowed_pairs(query_block, query_noisy, key_block, key_noisy):
    qb = query_block[:, None]
    kb = key_block[None, :]
    qn = query_noisy[:, None]
    kn = key_noisy[None, :]
    noisy_rows = qn & (kn & (kb == qb) | jnp.logical_not(kn) & (kb < qb))
    clean_rows = jnp.logical_not(qn) & jnp.logical_not(kn) & (kb <= qb)
    return noisy_rows | clean_rows


def block_rows(shard):
    return 2 * shard


def tile_grads(
    query_rows, grad_rows, norm_rows, delta_rows, key_rows, value_rows, mask, heads_here
):
    scale = HD ** (-0.5)
    query_count = query_rows.shape[0]
    key_count = key_rows.shape[0]
    width = query_rows.shape[1]
    query_three = query_rows.reshape(query_count, heads_here, HD)
    grad_three = grad_rows.reshape(query_count, heads_here, HD)
    key_three = key_rows.reshape(key_count, heads_here, HD)
    value_three = value_rows.reshape(key_count, heads_here, HD)
    score = jnp.einsum("qhd,khd->hqk", query_three, key_three, preferred_element_type=jnp.float32)
    norm = norm_rows.astype(jnp.float32).T[:, :, None]
    probs = jnp.where(mask[None], jnp.exp(score * scale - norm), 0.0)
    prob_grad = jnp.einsum(
        "qhd,khd->hqk", grad_three, value_three, preferred_element_type=jnp.float32
    )
    score_grad = (
        probs * (prob_grad - delta_rows.astype(jnp.float32).T[:, :, None]) * scale
    ).astype(jnp.bfloat16)
    query_add = None
    key_add = None
    value_add = None
    query_add = jnp.einsum(
        "hqk,khd->qhd", score_grad, key_three, preferred_element_type=jnp.float32
    ).reshape(query_count, width)
    probs_half = probs.astype(jnp.bfloat16)
    value_add = jnp.einsum(
        "hqk,qhd->khd", probs_half, grad_three, preferred_element_type=jnp.float32
    ).reshape(key_count, width)
    key_add = jnp.einsum(
        "hqk,qhd->khd", score_grad, query_three, preferred_element_type=jnp.float32
    ).reshape(key_count, width)
    return (query_add, key_add, value_add)


def unchanged(sums):
    return sums


def shards(queries, keys, values, attn_out, out_grad, out_weight, log_norm, block_sizes):
    rows_here = queries.shape[0]
    width = queries.shape[1]
    heads_here = width // HD
    devices = lax.axis_size("seq")
    place = lax.axis_index("seq")
    half = rows_here * devices // 2
    ends = jnp.cumsum(block_sizes)
    head_grad = lax.dot_general(
        lax.all_gather(out_grad, "head", axis=0, tiled=True),
        out_weight,
        (((1,), (1,)), ((), ())),
        preferred_element_type=jnp.float32,
    ).astype(jnp.bfloat16)
    delta = (
        (head_grad.astype(jnp.float32) * attn_out.astype(jnp.float32))
        .reshape(rows_here, heads_here, HD)
        .sum(-1)
        .astype(jnp.bfloat16)
    )

    def locate(first, count):
        position = first + jnp.arange(count, dtype=jnp.int32)
        return (block_index(position % half, ends), position < half, position >= half)

    own_block, own_noisy, own_clean = locate(place * rows_here, rows_here)
    key_sets = [(keys, values, own_block, own_noisy)]
    zero_rows = jnp.zeros((rows_here, width), jnp.float32)
    initial = [zero_rows for number in range(2 * len(key_sets))]
    initial.append(jnp.zeros((2 * half, width), jnp.float32))
    initial = tuple(initial)
    query_piece = lax.all_gather(queries, "seq", axis=0, tiled=True)
    grad_piece = lax.all_gather(head_grad, "seq", axis=0, tiled=True)
    norm_piece = lax.all_gather(log_norm, "seq", axis=0, tiled=True)
    delta_piece = lax.all_gather(delta, "seq", axis=0, tiled=True)
    count = query_piece.shape[0]
    unit = block_rows(rows_here)

    def one_block(index, inner):
        offset = index * unit
        query_rows = lax.dynamic_slice_in_dim(query_piece, offset, unit, 0)
        grad_rows = lax.dynamic_slice_in_dim(grad_piece, offset, unit, 0)
        norm_rows = lax.dynamic_slice_in_dim(norm_piece, offset, unit, 0)
        delta_rows = lax.dynamic_slice_in_dim(delta_piece, offset, unit, 0)
        query_block, query_noisy, query_clean = locate(offset, unit)
        updated = list(inner)
        query_total = jnp.zeros((unit, width), jnp.float32)
        for number, (key_rows, value_rows, key_block, key_noisy) in enumerate(key_sets):
            mask = allowed_pairs(query_block, query_noisy, key_block, key_noisy)

            def compute(sums, key_rows=key_rows, value_rows=value_rows, mask=mask):
                query_add, key_add, value_add = tile_grads(
                    query_rows,
                    grad_rows,
                    norm_rows,
                    delta_rows,
                    key_rows,
                    value_rows,
                    mask,
                    heads_here,
                )
                return (sums[0] + key_add, sums[1] + value_add, query_add)

            key_sum, value_sum, query_total = lax.cond(
                jnp.any(mask),
                compute,
                unchanged,
                (updated[2 * number], updated[2 * number + 1], query_total),
            )
            updated[2 * number] = key_sum
            updated[2 * number + 1] = value_sum
        current = lax.dynamic_slice_in_dim(updated[-1], offset, unit, 0)
        updated[-1] = lax.dynamic_update_slice_in_dim(updated[-1], current + query_total, offset, 0)
        return tuple(updated)

    folded = lax.fori_loop(0, count // unit, one_block, initial)
    key_grad = folded[0]
    value_grad = folded[1]
    query_grad = lax.psum_scatter(
        folded[-1].astype(jnp.bfloat16), "seq", scatter_dimension=0, tiled=True
    )
    return (query_grad, key_grad.astype(jnp.bfloat16), value_grad.astype(jnp.bfloat16))


def solution(mesh):
    in_specs = (
        P("seq", "head"),
        P("seq", "head"),
        P("seq", "head"),
        P("seq", "head"),
        P(("seq", "head"), None),
        P("head", None),
        P("seq", "head"),
        P(),
    )
    out_specs = (P("seq", "head"), P("seq", "head"), P("seq", "head"))
    return jax.shard_map(shards, mesh=mesh, in_specs=in_specs, out_specs=out_specs, check_vma=False)
```

profile of v0, /device:TPU:7, one launch (start us, length us, event | category | flops | bytes accessed | tf_op | source)
XLA Modules:
  0.0 673.4 jit_solution(3956577687125968423)
XLA Ops:
  11.0 56.6 %all-gather.6.cloned.1.call-done = bf16[512,4096]{1,0:T(8,128)(2,1)} async-done(((bf16[64,4096]{1,0:T(8,128)(2,1)}), bf16[512,4096]{1,0:T(8,128)(2,1)}) %all-gather.6.cloned.1.call-update) | async-done | bytes 4194320 | tf_op jit(solution)/shard_map/all_gather | solution.py:76
  67.6 4.2 bitcast_reduce_fusion
  72.4 24.4 %all_gather.16 = bf16[16384,2]{0,1:T(2,128)(2,1)S(1)} all-gather(bf16[512,2]{0,1:T(2,128)(2,1)S(1)} %copy-done.6), channel_id=1, replica_groups=mesh['seq'=32,'head'=8] {'seq'}, dimensions={0}, use_global_device_ids=true | all-gather | bytes 67584 | tf_op jit(solution)/shard_map/all_gather | solution.py:100
  97.2 22.0 %all_gather.19 = bf16[16384,2]{0,1:T(2,128)(2,1)S(1)} all-gather(bf16[512,2]{0,1:T(2,128)(2,1)S(1)} %get-tuple-element.572), channel_id=1, replica_groups=mesh['seq'=32,'head'=8] {'seq'}, dimensions={0}, use_global_device_ids=true | all-gather | bytes 67584 | tf_op jit(solution)/shard_map/all_gather | solution.py:101
  119.2 14.5 %all-gather.4.cloned.1.call-done = bf16[16384,256]{0,1:T(8,128)(2,1)} async-done(((bf16[512,256]{0,1:T(8,128)(2,1)}), bf16[16384,256]{0,1:T(8,128)(2,1)}) %all-gather.4.cloned.1.call-update) | async-done | bytes 8388624 | tf_op jit(solution)/shard_map/all_gather | solution.py:98
  133.7 67.4 %all-gather.8.cloned.1.call-done = bf16[16384,256]{0,1:T(8,128)(2,1)} async-done(((bf16[512,256]{0,1:T(8,128)(2,1)}), bf16[16384,256]{0,1:T(8,128)(2,1)}) %all-gather.8.cloned.1.call-update) | async-done | bytes 8388624 | tf_op jit(solution)/shard_map/all_gather | solution.py:99
  202.9 6.0 broadcast_in_dim.46.clone
  208.9 270.5 %while.21 = (s32[]{:T(128)}, f32[512,256]{0,1:T(8,128)}, f32[512,256]{0,1:T(8,128)}, f32[16384,256]{1,0:T(8,128)}, s32[512]{0:T(512)S(1)}, /*index=5*/s32[512]{0...) while((s32[]{:T(128)}, f32[512,256]{0,1:T(8,128)}, ...), condition=%wide.region_9.10_spmd.clone.clone, body=%wide.region_4.0_spmd.clone.clone.sunk | while | flops 1361596928 | bytes 49621980 | solution.py:142
  209.3 2.9 fusion.37
  212.9 2.3 constant_dynamic-slice_fusion.4
  221.1 2.9 fusion.37
  224.6 2.3 constant_dynamic-slice_fusion.4
  232.8 2.9 fusion.37
  236.4 2.3 constant_dynamic-slice_fusion.4
  244.6 2.9 fusion.37
  248.2 2.3 constant_dynamic-slice_fusion.4
  256.4 2.9 fusion.37
  259.9 2.3 constant_dynamic-slice_fusion.4
  263.8 10.4 %conditional.4 = (f32[512,256]{0,1:T(8,128)}, f32[512,256]{0,1:T(8,128)}, f32[1024,256]{0,1:T(8,128)S(1)}) conditional(s32[]{:T(128)} %convert_element_type.85, (f32[512,256]{0,1:T(8,128)}, f32[512,256]{0,1:T(8,128)}) %tuple.77, (pred[1024,512]{1,0:T(8,128)(4,1)}, bf16[16384,256]{0,1:T(8,128)(2,1)}, s32[]{:T(128)}, bf16[512,256]{0,1:T(8,128)(2,1)S(1)}, ...), branch_computations={%region_7.7_spmd, %region_8.8_spmd} | conditional | flops 1353977856 | bytes 37535896 | solution.py:130
  278.4 2.9 fusion.37
  282.0 2.3 constant_dynamic-slice_fusion.4
  285.8 10.4 %conditional.4 = (f32[512,256]{0,1:T(8,128)}, f32[512,256]{0,1:T(8,128)}, f32[1024,256]{0,1:T(8,128)S(1)}) conditional(s32[]{:T(128)} %convert_element_type.85, (f32[512,256]{0,1:T(8,128)}, f32[512,256]{0,1:T(8,128)}) %tuple.77, (pred[1024,512]{1,0:T(8,128)(4,1)}, bf16[16384,256]{0,1:T(8,128)(2,1)}, s32[]{:T(128)}, bf16[512,256]{0,1:T(8,128)(2,1)S(1)}, ...), branch_computations={%region_7.7_spmd, %region_8.8_spmd} | conditional | flops 1353977856 | bytes 37535896 | solution.py:130
  300.5 2.9 fusion.37
  304.0 2.3 constant_dynamic-slice_fusion.4
  307.9 10.4 %conditional.4 = (f32[512,256]{0,1:T(8,128)}, f32[512,256]{0,1:T(8,128)}, f32[1024,256]{0,1:T(8,128)S(1)}) conditional(s32[]{:T(128)} %convert_element_type.85, (f32[512,256]{0,1:T(8,128)}, f32[512,256]{0,1:T(8,128)}) %tuple.77, (pred[1024,512]{1,0:T(8,128)(4,1)}, bf16[16384,256]{0,1:T(8,128)(2,1)}, s32[]{:T(128)}, bf16[512,256]{0,1:T(8,128)(2,1)S(1)}, ...), branch_computations={%region_7.7_spmd, %region_8.8_spmd} | conditional | flops 1353977856 | bytes 37535896 | solution.py:130
  322.5 2.9 fusion.37
  326.1 2.3 constant_dynamic-slice_fusion.4
  329.9 10.4 %conditional.4 = (f32[512,256]{0,1:T(8,128)}, f32[512,256]{0,1:T(8,128)}, f32[1024,256]{0,1:T(8,128)S(1)}) conditional(s32[]{:T(128)} %convert_element_type.85, (f32[512,256]{0,1:T(8,128)}, f32[512,256]{0,1:T(8,128)}) %tuple.77, (pred[1024,512]{1,0:T(8,128)(4,1)}, bf16[16384,256]{0,1:T(8,128)(2,1)}, s32[]{:T(128)}, bf16[512,256]{0,1:T(8,128)(2,1)S(1)}, ...), branch_computations={%region_7.7_spmd, %region_8.8_spmd} | conditional | flops 1353977856 | bytes 37535896 | solution.py:130
  344.6 2.9 fusion.37
  348.1 2.3 constant_dynamic-slice_fusion.4
  356.4 2.9 fusion.37
  359.9 2.3 constant_dynamic-slice_fusion.4
  368.1 2.9 fusion.37
  371.7 2.3 constant_dynamic-slice_fusion.4
  379.9 2.9 fusion.37
  383.4 2.3 constant_dynamic-slice_fusion.4
  391.6 2.9 fusion.37
  395.2 2.3 constant_dynamic-slice_fusion.4
  399.0 10.4 %conditional.4 = (f32[512,256]{0,1:T(8,128)}, f32[512,256]{0,1:T(8,128)}, f32[1024,256]{0,1:T(8,128)S(1)}) conditional(s32[]{:T(128)} %convert_element_type.85, (f32[512,256]{0,1:T(8,128)}, f32[512,256]{0,1:T(8,128)}) %tuple.77, (pred[1024,512]{1,0:T(8,128)(4,1)}, bf16[16384,256]{0,1:T(8,128)(2,1)}, s32[]{:T(128)}, bf16[512,256]{0,1:T(8,128)(2,1)S(1)}, ...), branch_computations={%region_7.7_spmd, %region_8.8_spmd} | conditional | flops 1353977856 | bytes 37535896 | solution.py:130
  413.7 2.9 fusion.37
  417.3 2.3 constant_dynamic-slice_fusion.4
  421.1 10.4 %conditional.4 = (f32[512,256]{0,1:T(8,128)}, f32[512,256]{0,1:T(8,128)}, f32[1024,256]{0,1:T(8,128)S(1)}) conditional(s32[]{:T(128)} %convert_element_type.85, (f32[512,256]{0,1:T(8,128)}, f32[512,256]{0,1:T(8,128)}) %tuple.77, (pred[1024,512]{1,0:T(8,128)(4,1)}, bf16[16384,256]{0,1:T(8,128)(2,1)}, s32[]{:T(128)}, bf16[512,256]{0,1:T(8,128)(2,1)S(1)}, ...), branch_computations={%region_7.7_spmd, %region_8.8_spmd} | conditional | flops 1353977856 | bytes 37535896 | solution.py:130
  435.7 2.9 fusion.37
  443.1 10.4 %conditional.4 = (f32[512,256]{0,1:T(8,128)}, f32[512,256]{0,1:T(8,128)}, f32[1024,256]{0,1:T(8,128)S(1)}) conditional(s32[]{:T(128)} %convert_element_type.85, (f32[512,256]{0,1:T(8,128)}, f32[512,256]{0,1:T(8,128)}) %tuple.77, (pred[1024,512]{1,0:T(8,128)(4,1)}, bf16[16384,256]{0,1:T(8,128)(2,1)}, s32[]{:T(128)}, bf16[512,256]{0,1:T(8,128)(2,1)S(1)}, ...), branch_computations={%region_7.7_spmd, %region_8.8_spmd} | conditional | flops 1353977856 | bytes 37535896 | solution.py:130
  457.8 2.9 fusion.37
  465.2 10.4 %conditional.4 = (f32[512,256]{0,1:T(8,128)}, f32[512,256]{0,1:T(8,128)}, f32[1024,256]{0,1:T(8,128)S(1)}) conditional(s32[]{:T(128)} %convert_element_type.85, (f32[512,256]{0,1:T(8,128)}, f32[512,256]{0,1:T(8,128)}) %tuple.77, (pred[1024,512]{1,0:T(8,128)(4,1)}, bf16[16384,256]{0,1:T(8,128)(2,1)}, s32[]{:T(128)}, bf16[512,256]{0,1:T(8,128)(2,1)S(1)}, ...), branch_computations={%region_7.7_spmd, %region_8.8_spmd} | conditional | flops 1353977856 | bytes 37535896 | solution.py:130
  479.4 8.9 %convert_element_type.65 = bf16[16384,256]{1,0:T(8,128)(2,1)} convert(f32[16384,256]{1,0:T(8,128)} %get-tuple-element.428) | non-fusion elementwise | flops 4194304 | bytes 25165824 | tf_op jit(solution)/shard_map/convert_element_type | solution.py:146
  492.1 174.8 %reduce-scatter.2.cloned.1.call-done = bf16[512,256]{1,0:T(8,128)(2,1)} async-done(((bf16[16384,256]{1,0:T(8,128)(2,1)}), bf16[512,256]{1,0:T(8,128)(2,1)}) %reduce-scatter.2.cloned.1.call-update) | async-done | bytes 262160 | tf_op jit(solution)/shard_map/reduce_scatter | solution.py:145
  (338 shorter events, 191.0 us)
Async XLA Ops:
  7.2 60.4 %copy-start = (bf16[256,4096]{1,0:T(8,128)(2,1)S(1)}, bf16[256,4096]{1,0:T(8,128)(2,1)}, u32[]{:S(2)}) copy-start(bf16[256,4096]{1,0:T(8,128)(2,1)} %param.17) | copy-start | bytes 6291460
  7.2 60.4 %all-gather.6.cloned.1.call-start = ((), (), s32[]{:S(2)}) async-start(), calls=%async_computation.2 | async-start | bytes 4718592 | tf_op jit(solution)/shard_map/all_gather | solution.py:76
  7.9 125.8 %all-gather.4.cloned.1.call-start = ((), (), s32[]{:S(2)}) async-start(), calls=%async_computation.1 | async-start | bytes 8650752 | tf_op jit(solution)/shard_map/all_gather | solution.py:98
  9.8 191.3 %all-gather.8.cloned.1.call-start = ((), (), s32[]{:S(2)}) async-start(), calls=%async_computation.3 | async-start | bytes 8650752 | tf_op jit(solution)/shard_map/all_gather | solution.py:99
  10.9 60.9 %copy-start.7 = (s32[512]{0:T(512)S(1)}, s32[512]{0:T(512)}, u32[]{:S(2)}) copy-start(s32[512]{0:T(512)} %param.19) | copy-start | bytes 6148
  10.9 61.3 %copy-start.5 = (bf16[512,256]{1,0:T(8,128)(2,1)S(1)}, bf16[512,256]{1,0:T(8,128)(2,1)}, u32[]{:S(2)}) copy-start(bf16[512,256]{1,0:T(8,128)(2,1)} %param.13) | copy-start | bytes 786436
  11.0 61.4 %copy-start.6 = (bf16[512,2]{0,1:T(2,128)(2,1)S(1)}, bf16[512,2]{0,1:T(2,128)(2,1)}, u32[]{:S(2)}) copy-start(bf16[512,2]{0,1:T(2,128)(2,1)} %param.18) | copy-start | bytes 6148
  71.8 595.1 %reduce-scatter.2.cloned.1.call-start = ((), (), s32[]{:S(2)}) async-start(), calls=%async_computation.4 | async-start | bytes 8650752 | tf_op jit(solution)/shard_map/reduce_scatter | solution.py:145
  263.8 3.0 copy-start.4
  266.8 1.2 copy-start.8
  270.0 1.3 copy-start.1
  273.4 0.8 copy-start.2
  285.8 3.0 copy-start.4
  288.9 1.2 copy-start.8
  292.1 1.3 copy-start.1
  295.4 0.8 copy-start.2
  307.9 3.0 copy-start.4
  310.9 1.2 copy-start.8
  314.1 1.3 copy-start.1
  317.5 0.8 copy-start.2
  329.9 3.0 copy-start.4
  333.0 1.2 copy-start.8
  336.2 1.3 copy-start.1
  339.6 0.8 copy-start.2
  399.0 3.0 copy-start.4
  402.1 1.2 copy-start.8
  405.3 1.3 copy-start.1
  408.6 0.8 copy-start.2
  421.1 3.0 copy-start.4
  424.2 1.2 copy-start.8
  427.4 1.3 copy-start.1
  430.7 0.8 copy-start.2
  443.2 3.0 copy-start.4
  446.2 1.2 copy-start.8
  449.4 1.3 copy-start.1
  452.8 0.8 copy-start.2
  465.2 3.0 copy-start.4
  468.3 1.2 copy-start.8
  471.5 1.3 copy-start.1
  474.9 0.8 copy-start.2
  488.3 1.0 copy-start.3
Sparse Core Ops, SparseCore 0:
  9.8 57.7 all-gather.5
  70.6 63.0 all-gather.3
  136.7 64.3 all-gather.7
  488.4 178.3 reduce-scatter.1
where the time goes:
time: 679 us; the launch traced here: 673 us
  waiting for transfers between devices  314 us (46%)
  local copies, waits for them, and re-layouts  143 us (21%)
  other arithmetic  98 us (14%)
  blocking collectives  46.3 us (7%)
  matrix products  45.6 us (7%)
  between operations  13.8 us (2%)
  loops' own time  12.3 us (2%)
    reduce_scatter x1, waiting for transfers between devices, shards(): lax.psum_scatter(folded[-1].astype(jnp.bfloat16), 'seq', scatter_dimensio...  175 us
    all_gather x1, waiting for transfers between devices, shards(): grad_piece = lax.all_gather(head_grad, 'seq', axis=0, tiled=True)  67.4 us
    dynamic_slice x32, local copies, waits for them, and re-layouts, one_block(): current = lax.dynamic_slice_in_dim(updated[-1], offset, unit, 0)  61.3 us
    all_gather x1, waiting for transfers between devices, shards(): lax.all_gather(out_grad, 'head', axis=0, tiled=True)  56.6 us
    reduce_or x16, other arithmetic, one_block(): jnp.any(mask)  46.7 us
    dynamic_update_slice x32, local copies, waits for them, and re-layouts, one_block(): lax.dynamic_update_slice_in_dim(updated[-1], current + query_total, offse...  41.9 us
    all_gather x1, blocking collectives, shards(): norm_piece = lax.all_gather(log_norm, 'seq', axis=0, tiled=True)  24.4 us
    all_gather x1, blocking collectives, shards(): delta_piece = lax.all_gather(delta, 'seq', axis=0, tiled=True)  22 us
  transfers between devices with their start and end apart: 4, of which 4 were waited for; matrix products, arithmetic and copies ran while one was open for 2% of the time, Pallas kernels for 0%

commit v1 on v0

v1 whole, which is shorter than its diff:
```python
import functools
import math

import jax
import jax.numpy as jnp
from jax import lax
from jax.experimental import pallas as pl
from jax.experimental.pallas import tpu as pltpu
from jax.sharding import PartitionSpec as P

HD = 128
UNIT = 32
ROWS = 512
STRIPE = 128
TASK_Q = 4096
TASK_K = 2048
PEERS = 32
SHARDS = 16
SCALE = HD ** -0.5
MESH = pl.DeviceIdType.MESH
F32 = jnp.float32
BF16 = jnp.bfloat16
CONTRACT_LAST = (((1,), (1,)), ((), ()))
CONTRACT_FIRST = (((0,), (0,)), ((), ()))


def where_am_i():
    seq = lax.axis_index("seq")
    x, y, core = seq // 8, (seq // 2) % 4, seq % 2
    return seq, x, y, core


def own_rows(seq):
    x, y, core = seq // 8, (seq // 2) % 4, seq % 2
    slot = x % 2
    group = y + slot * (3 - 2 * y)
    return group, slot * 2048 + (x // 2) * 1024 + core * ROWS


def multiple(value, of):
    return pl.multiple_of(value, of)


def push(here, there, device, me, send_sem, recv_sem):
    seq, head = device

    @pl.when(seq == me)
    def _():
        pltpu.make_async_copy(here, there, recv_sem).start()

    @pl.when(seq != me)
    def _():
        pltpu.make_async_remote_copy(
            src_ref=here, dst_ref=there, send_sem=send_sem, recv_sem=recv_sem,
            device_id=(seq, head), device_id_type=MESH,
        ).start()


def wait_bytes(ref, sem):
    pltpu.make_async_copy(ref, ref, sem).wait()


def greet_plane(barrier, me, head):
    def greet(step, carry):
        pl.semaphore_signal(
            barrier, inc=1, device_id=(lax.rem(me + step, PEERS), head), device_id_type=MESH
        )
        return carry

    lax.fori_loop(1, PEERS, greet, 0)


def spread_kernel(
    q_ref, k_ref, v_ref, o_ref, g_ref, w_ref, n_ref,
    qg, dg, kg, vg, dl,
    from_left, from_right,
    ring_send, ring_recv, q_send, k_send, v_send, d_send, q_recv, k_recv, v_recv, d_recv,
):
    me, x, y, core = where_am_i()
    head = lax.axis_index("head")
    right, left = lax.rem(head + 1, 8), lax.rem(head + 7, 8)
    group, row0 = own_rows(me)
    place = me % SHARDS
    clean = me >= SHARDS

    barrier = pltpu.get_barrier_semaphore()
    greet_plane(barrier, me, head)
    for neighbour in (left, right):
        pl.semaphore_signal(barrier, inc=1, device_id=(me, neighbour), device_id_type=MESH)
    pl.semaphore_wait(barrier, PEERS + 1)

    def ring(direction, index):
        landed = (from_left, from_right)[direction]
        if index < 2:
            unit = index if direction == 0 else 1 - index
            source = g_ref.at[pl.ds(unit * UNIT, UNIT)]
        else:
            source = landed.at[index - 2]
        return pltpu.make_async_remote_copy(
            src_ref=source,
            dst_ref=landed.at[index],
            send_sem=ring_send.at[direction, index],
            recv_sem=ring_recv.at[direction, index],
            device_id=(me, (right, left)[direction]),
            device_id_type=MESH,
        )

    for index in range(2):
        for direction in range(2):
            ring(direction, index).start()

    def task_of(index):
        return (index // 2 * 4 + group) * 2 + index % 2

    def send_queries(step, carry):
        index = lax.rem(me + step, 8)
        column = multiple(index % 2 * HD, HD)
        push(
            q_ref.at[:, pl.ds(column, HD)],
            qg.at[pl.ds(multiple(row0, ROWS), ROWS)],
            (task_of(index), head), me, q_send.at[index], q_recv,
        )
        return carry

    lax.fori_loop(0, 8, send_queries, 0)

    @pl.when(clean)
    def _():
        def send_keys(step, carry):
            device = lax.rem(me + step, PEERS)
            row = multiple(device // 8 * STRIPE, STRIPE)
            column = multiple(device % 2 * HD, HD)
            target = pl.ds(multiple(place * STRIPE, STRIPE), STRIPE)
            for source, landed, send, recv in ((k_ref, kg, k_send, k_recv), (v_ref, vg, v_send, v_recv)):
                push(
                    source.at[pl.ds(row, STRIPE), pl.ds(column, HD)],
                    landed.at[target],
                    (device, head), me, send.at[device], recv,
                )
            return carry

        lax.fori_loop(0, PEERS, send_keys, 0)

    lane = lax.broadcasted_iota(jnp.int32, (UNIT, HD), 1)

    def produce(unit_ref, owner, unit):
        start = multiple(owner * 64 + unit * UNIT, UNIT)
        rows = pl.ds(start, UNIT)
        grad = lax.dot_general(
            unit_ref[...], w_ref[...], CONTRACT_LAST, preferred_element_type=F32
        ).astype(BF16)
        for h in range(2):
            columns = slice(h * HD, (h + 1) * HD)
            part = grad[:, columns]
            delta = jnp.sum(
                part.astype(F32) * o_ref[rows, columns].astype(F32), axis=1, keepdims=True
            ).astype(BF16)
            norm = n_ref[rows, :].astype(F32)[:, h:h + 1] * (1.0 / SCALE)
            high = norm.astype(BF16)
            rest = norm - high.astype(F32)
            middle = rest.astype(BF16)
            low = (rest - middle.astype(F32)).astype(BF16)
            extra = jnp.where(lane == 0, high.astype(F32), 0.0)
            extra = jnp.where(lane == 1, middle.astype(F32), extra)
            extra = jnp.where(lane == 2, low.astype(F32), extra)
            extra = jnp.where(lane == 3, delta.astype(F32), extra)
            dl[rows, h * 256:h * 256 + HD] = part
            dl[rows, h * 256 + HD:(h + 1) * 256] = extra.astype(BF16)

        def send(step, carry):
            index = lax.rem(me + step, 8)
            column = multiple(index % 2 * 256, 256)
            push(
                dl.at[rows, pl.ds(column, 256)],
                dg.at[pl.ds(multiple(row0 + start, UNIT), UNIT)],
                (task_of(index), head), me, d_send.at[index], d_recv,
            )
            return carry

        lax.fori_loop(0, 8, send, 0)

    for unit in range(2):
        produce(g_ref.at[pl.ds(unit * UNIT, UNIT)], head, unit)
    for index in range(7):
        for direction in range(2):
            ring(direction, index).wait_recv()
            if index < 5:
                ring(direction, index + 2).start()
        away = index // 2 + 1
        produce(from_left.at[index], lax.rem(head + 8 - away, 8), index % 2)
        produce(from_right.at[index], lax.rem(head + away, 8), 1 - index % 2)

    wait_bytes(dg, d_recv)
    wait_bytes(qg, q_recv)
    wait_bytes(kg, k_recv)
    wait_bytes(vg, v_recv)
    for index in range(7):
        for direction in range(2):
            ring(direction, index).wait_send()

    def settle(index, carry):
        @pl.when(task_of(index) != me)
        def _():
            wait_bytes(q_ref.at[:, pl.ds(0, HD)], q_send.at[index])
            wait_bytes(dl.at[:, pl.ds(0, 256)], d_send.at[index])
        return carry

    lax.fori_loop(0, 8, settle, 0)

    @pl.when(clean)
    def _():
        def settle_keys(step, carry):
            device = lax.rem(me + step, PEERS)
            wait_bytes(k_ref.at[pl.ds(0, STRIPE), pl.ds(0, HD)], k_send.at[device])
            wait_bytes(v_ref.at[pl.ds(0, STRIPE), pl.ds(0, HD)], v_send.at[device])
            return carry

        lax.fori_loop(1, PEERS, settle_keys, 0)


def dot(a, b, dims):
    return lax.dot_general(a, b, dims, preferred_element_type=F32)


def pick(shape, first, last):
    lane = lax.broadcasted_iota(jnp.int32, shape, 1)
    return jnp.where((lane >= first) & (lane <= last), -1.0, 0.0).astype(BF16)


def tile(q, d, k, v, mask):
    rows = k.shape[0]
    keys = jnp.concatenate([k, pick((rows, HD), 0, 2)], axis=1)
    values = jnp.concatenate([v, pick((rows, HD), 3, 3)], axis=1)
    score = dot(jnp.concatenate([q, d[:, HD:]], axis=1), keys, CONTRACT_LAST)
    probs = jnp.exp2(score * (SCALE * math.log2(math.e)))
    if mask is not None:
        probs = jnp.where(mask, probs, 0.0)
    grad = (probs * dot(d, values, CONTRACT_LAST)).astype(BF16)
    dq = dot(grad, k, (((1,), (0,)), ((), ())))
    dk = dot(grad, q, CONTRACT_FIRST)
    dv = dot(probs.astype(BF16), d[:, :HD], CONTRACT_FIRST)
    return dq, dk, dv


TILE_Q = 512


def attend_kernel(
    sizes, qg, dg, kg, vg, q_ref, k_ref, v_ref, dl,
    dq_out, dk_out, dv_out, dq_own, dk_own, dv_own,
    dq_sum, dk_sum, dv_sum, row_block, own_block,
):
    me, x, y, core = where_am_i()
    group, stripe = y, x
    place = me % SHARDS
    dq_sum[...] = jnp.zeros_like(dq_sum)
    dk_sum[...] = jnp.zeros_like(dk_sum)
    dv_sum[...] = jnp.zeros_like(dv_sum)

    def coarse_of(slot):
        return group + slot * (7 - 2 * group)

    in_group = lax.broadcasted_iota(jnp.int32, (32, HD), 0)

    def number_rows(index, carry):
        pair = coarse_of(index // 32) * 32 + index % 32
        row_block[pl.ds(multiple(index * 32, 32), 32), :] = 2 * pair + jnp.where(
            in_group >= sizes[2 * pair], 1, 0
        )
        return carry

    lax.fori_loop(0, 64, number_rows, 0)

    lane = lax.broadcasted_iota(jnp.int32, (1, HD), 1)

    def key_blocks(coarse, half):
        pair = (coarse * 1024 + half * ROWS + stripe * STRIPE) // 32
        part = lane // 32
        size = jnp.where(
            part < 2,
            jnp.where(part == 0, sizes[2 * pair], sizes[2 * pair + 2]),
            jnp.where(part == 2, sizes[2 * pair + 4], sizes[2 * pair + 6]),
        )
        return 2 * (pair + part) + jnp.where(lane % 32 >= size, 1, 0)

    def step(slot, pair, blocks):
        keys = pl.ds(multiple(pair * 256, 256), 256)

        def inner(index, carry):
            rows = pl.ds(multiple(slot * 2048 + index * TILE_Q, TILE_Q), TILE_Q)
            mask = None
            if blocks is not None:
                per = 1024 // TILE_Q
                start = multiple(slot * 1024 + index % per * TILE_Q, TILE_Q)
                own = row_block[pl.ds(start, TILE_Q), :] + index // per
                mask = jnp.concatenate([own, own], axis=1) > blocks
            dq, dk, dv = tile(qg[rows, :], dg[rows, :], kg[keys, :], vg[keys, :], mask)
            dq_sum[rows, :] += dq
            dk_sum[keys, :] += dk
            dv_sum[keys, :] += dv
            return carry

        lax.fori_loop(0, 2048 // TILE_Q, inner, 0)

    for slot in range(2):
        coarse = coarse_of(slot)

        def full(pair, carry):
            step(slot, pair, None)
            return carry

        lax.fori_loop(0, coarse, full, 0)
        step(slot, coarse, jnp.concatenate([key_blocks(coarse, 0), key_blocks(coarse, 1)], axis=1))

    dq_out[...] = (dq_sum[...] * SCALE).astype(BF16)
    dk_out[...] = (dk_sum[...] * SCALE).astype(BF16)
    dv_out[...] = dv_sum[...].astype(BF16)

    @pl.when(me < SHARDS)
    def _():
        def number_own(index, carry):
            pair = place * 16 + index
            own_block[pl.ds(multiple(index * 32, 32), 32), :] = 2 * pair + jnp.where(
                in_group >= sizes[2 * pair], 1, 0
            )
            return carry

        lax.fori_loop(0, 16, number_own, 0)
        for part in range(4):
            rows = slice(part * STRIPE, (part + 1) * STRIPE)
            block = own_block[rows, :].astype(F32)
            mask = block == block.T
            for h in range(2):
                columns = slice(h * HD, (h + 1) * HD)
                dq, dk, dv = tile(
                    q_ref[rows, columns], dl[rows, h * 256:(h + 1) * 256],
                    k_ref[rows, columns], v_ref[rows, columns], mask,
                )
                dq_own[rows, columns] = (dq * SCALE).astype(BF16)
                dk_own[rows, columns] = (dk * SCALE).astype(BF16)
                dv_own[rows, columns] = dv.astype(BF16)


def collect_kernel(
    dq, dk, dv, dq_own, dk_own, dv_own,
    dq_out, dk_out, dv_out,
    rq, rk, rv,
    q_send, k_send, v_send, q_recv, k_recv, v_recv,
):
    me, x, y, core = where_am_i()
    head = lax.axis_index("head")
    clean = me >= SHARDS
    barrier = pltpu.get_barrier_semaphore()
    greet_plane(barrier, me, head)
    pl.semaphore_wait(barrier, PEERS - 1)
    columns = pl.ds(multiple(core * HD, HD), HD)

    def query_owner(index):
        slot, kind, half = index // 4, index // 2 % 2, index % 2
        coarse = y + slot * (7 - 2 * y)
        return kind * SHARDS + 2 * coarse + half

    def send_queries(step, carry):
        index = lax.rem(me + step, 8)
        push(
            dq.at[pl.ds(multiple(index * ROWS, ROWS), ROWS)],
            rq.at[x, :, columns],
            (query_owner(index), head), me, q_send.at[index], q_recv,
        )
        return carry

    def send_keys(step, carry):
        index = lax.rem(me + step, SHARDS)
        rows = pl.ds(multiple(index * STRIPE, STRIPE), STRIPE)
        target = pl.ds(multiple(x * STRIPE, STRIPE), STRIPE)
        for source, landed, send, recv in ((dk, rk, k_send, k_recv), (dv, rv, v_send, v_recv)):
            push(
                source.at[rows],
                landed.at[y, target, columns],
                (SHARDS + index, head), me, send.at[index], recv,
            )
        return carry

    lax.fori_loop(0, SHARDS, send_keys, 0)
    lax.fori_loop(0, 8, send_queries, 0)

    wait_bytes(rq, q_recv)

    @pl.when(clean)
    def _():
        dq_out[...] = (
            (rq[0].astype(F32) + rq[1].astype(F32)) + (rq[2].astype(F32) + rq[3].astype(F32))
        ).astype(BF16)
        wait_bytes(rk, k_recv)
        wait_bytes(rv, v_recv)
        for landed, out in ((rk, dk_out), (rv, dv_out)):
            out[...] = (
                (landed[0].astype(F32) + landed[1].astype(F32))
                + (landed[2].astype(F32) + landed[3].astype(F32))
            ).astype(BF16)

    @pl.when(me < SHARDS)
    def _():
        dq_out[...] = (
            (rq[0].astype(F32) + rq[1].astype(F32)) + (rq[2].astype(F32) + rq[3].astype(F32))
            + dq_own[...].astype(F32)
        ).astype(BF16)
        dk_out[...] = dk_own[...]
        dv_out[...] = dv_own[...]

    def settle_queries(index, carry):
        @pl.when(query_owner(index) != me)
        def _():
            wait_bytes(dq.at[pl.ds(0, ROWS)], q_send.at[index])
        return carry

    lax.fori_loop(0, 8, settle_queries, 0)

    def settle_keys(index, carry):
        @pl.when(SHARDS + index != me)
        def _():
            wait_bytes(dk.at[pl.ds(0, STRIPE)], k_send.at[index])
            wait_bytes(dv.at[pl.ds(0, STRIPE)], v_send.at[index])
        return carry

    lax.fori_loop(0, SHARDS, settle_keys, 0)


ANY = pl.BlockSpec(memory_space=pl.ANY)
VMEM = pl.BlockSpec(memory_space=pltpu.VMEM)
SMEM = pl.BlockSpec(memory_space=pltpu.SMEM)
DMA = pltpu.SemaphoreType.DMA
LIMIT = 56 * 1024 * 1024


def half_array(*shape):
    return jax.ShapeDtypeStruct(shape, BF16)


def spread(queries, keys, values, attn_out, out_grad, out_weight, log_norm):
    return pl.pallas_call(
        spread_kernel,
        name="spread",
        out_shape=(
            half_array(TASK_Q, HD), half_array(TASK_Q, 256), half_array(TASK_K, HD),
            half_array(TASK_K, HD), half_array(ROWS, 512),
        ),
        in_specs=[ANY, ANY, ANY, VMEM, VMEM, VMEM, VMEM],
        out_specs=(ANY, ANY, ANY, ANY, VMEM),
        scratch_shapes=[
            pltpu.VMEM((7, UNIT, 4096), BF16),
            pltpu.VMEM((7, UNIT, 4096), BF16),
            DMA((2, 7)), DMA((2, 7)), DMA((8,)), DMA((PEERS,)), DMA((PEERS,)), DMA((8,)),
            DMA, DMA, DMA, DMA,
        ],
        compiler_params=pltpu.CompilerParams(
            collective_id=0, has_side_effects=True, vmem_limit_bytes=LIMIT
        ),
    )(queries, keys, values, attn_out, out_grad, out_weight, log_norm)


def attend(block_sizes, spread_out, queries, keys, values):
    qg, dg, kg, vg, dl = spread_out
    return pl.pallas_call(
        attend_kernel,
        name="attend",
        out_shape=(
            half_array(TASK_Q, HD), half_array(TASK_K, HD), half_array(TASK_K, HD),
            half_array(ROWS, 256), half_array(ROWS, 256), half_array(ROWS, 256),
        ),
        in_specs=[SMEM] + [VMEM] * 8,
        out_specs=(VMEM,) * 6,
        scratch_shapes=[
            pltpu.VMEM((TASK_Q, HD), F32),
            pltpu.VMEM((TASK_K, HD), F32),
            pltpu.VMEM((TASK_K, HD), F32),
            pltpu.VMEM((2048, HD), jnp.int32),
            pltpu.VMEM((ROWS, HD), jnp.int32),
        ],
        compiler_params=pltpu.CompilerParams(vmem_limit_bytes=LIMIT),
    )(block_sizes, qg, dg, kg, vg, queries, keys, values, dl)


def collect(parts):
    return pl.pallas_call(
        collect_kernel,
        name="collect",
        out_shape=(half_array(ROWS, 256),) * 3,
        in_specs=[VMEM] * 6,
        out_specs=(VMEM,) * 3,
        scratch_shapes=[
            pltpu.VMEM((4, ROWS, 256), BF16),
            pltpu.VMEM((4, ROWS, 256), BF16),
            pltpu.VMEM((4, ROWS, 256), BF16),
            DMA((8,)), DMA((SHARDS,)), DMA((SHARDS,)),
            DMA, DMA, DMA,
        ],
        compiler_params=pltpu.CompilerParams(
            collective_id=1, has_side_effects=True, vmem_limit_bytes=LIMIT
        ),
    )(*parts)


def shards(queries, keys, values, attn_out, out_grad, out_weight, log_norm, block_sizes):
    moved = spread(queries, keys, values, attn_out, out_grad, out_weight, log_norm)
    parts = attend(block_sizes, moved, queries, keys, values)
    return collect(parts)


def solution(mesh):
    in_specs = (
        P("seq", "head"),
        P("seq", "head"),
        P("seq", "head"),
        P("seq", "head"),
        P(("seq", "head"), None),
        P("head", None),
        P("seq", "head"),
        P(),
    )
    out_specs = (P("seq", "head"), P("seq", "head"), P("seq", "head"))
    return jax.shard_map(shards, mesh=mesh, in_specs=in_specs, out_specs=out_specs, check_vma=False)
```

time: 679 us -> 168 us (0.25)
  waiting for transfers between devices: 314 us -> 0 us
  Pallas kernels: 0 us -> 159 us
  local copies, waits for them, and re-layouts: 143 us -> 6.5 us
  other arithmetic: 98 us -> 0 us
  blocking collectives: 46.3 us -> 0 us
  matrix products: 45.6 us -> 0 us
  between operations: 13.8 us -> 0.65 us
  loops' own time: 12.3 us -> 0 us
    reduce_scatter x1 -> x0, waiting for transfers between devices: 175 us -> none  [shards(): lax.psum_scatter(folded[-1].astype(jnp.bfloat16), 'seq', scatter_dimensio...]
    pallas_call x0 -> x3, Pallas kernels: none -> 159 us  [the longest x1 68.2 us: spread(): pl.pallas_call(spread_kernel, name='spread', out_shape=(half_array(TASK_Q...]
    all_gather x3 -> x0, waiting for transfers between devices: 139 us -> none  [the longest x1 67.4 us: shards(): grad_piece = lax.all_gather(head_grad, 'seq', axis=0, tiled=True)]
    dynamic_slice x48 -> x0, local copies, waits for them, and re-layouts: 79.1 us -> none  [the longest x32 61.3 us: one_block(): current = lax.dynamic_slice_in_dim(updated[-1], offset, unit, 0)]
    reduce_or x16 -> x0, other arithmetic: 46.7 us -> none  [one_block(): jnp.any(mask)]
    all_gather x2 -> x0, blocking collectives: 46.3 us -> none  [the longest x1 24.4 us: shards(): norm_piece = lax.all_gather(log_norm, 'seq', axis=0, tiled=True)]
    dot_general x41 -> x0, matrix products: 45.6 us -> none  [the longest x8 15.9 us: tile_grads(): jnp.einsum('qhd,khd->hqk', grad_three, value_three, preferred_element_typ...]
    dynamic_update_slice x32 -> x0, local copies, waits for them, and re-layouts: 41.9 us -> none  [one_block(): lax.dynamic_update_slice_in_dim(updated[-1], current + query_total, offse...]
  transfers between devices with their start and end apart: 4 -> 0, of which waited for: 4 -> 0; matrix products, arithmetic and copies ran while one was open for 2% -> 0% of each run, Pallas kernels for 0% -> 0%
where the time goes in v1:
time: 168 us; the launch traced here: 166 us
  Pallas kernels  159 us (95%)
  local copies, waits for them, and re-layouts  6.5 us (4%)
    pallas_call x1, Pallas kernels, spread(): pl.pallas_call(spread_kernel, name='spread', out_shape=(half_array(TASK_Q...  68.2 us
    pallas_call x1, Pallas kernels, collect(): pl.pallas_call(collect_kernel, name='collect', out_shape=(half_array(ROWS...  62 us
    pallas_call x1, Pallas kernels, attend(): pl.pallas_call(attend_kernel, name='attend', out_shape=(half_array(TASK_Q...  28.8 us
    unnamed x4, local copies, waits for them, and re-layouts  6.5 us

profile of v1, /device:TPU:7, one launch (start us, length us, event | category | flops | bytes accessed | tf_op | source)
XLA Modules:
  0.0 166.1 jit_solution(7430965266697483095)
XLA Ops:
  0.6 1.5 copy.11.n_ref
  2.1 68.2 %spread.1 = (bf16[4096,128]{1,0:T(8,128)(2,1)}, bf16[4096,256]{1,0:T(8,128)(2,1)}, bf16[2048,128]{1,0:T(8,128)(2,1)}, bf16[2048,128]{1,0:T(8,128)(2,1)}, bf16[512,512]{1,0:T(8,128)(2,1)}) custom-call(bf16[512,256]{1,0:T(8,128)(2,1)} %q_ref.3, bf16[512,256]{1,0:T(8,128)(2,1)} %k_ref.3, bf16[512,256]{1,0:T(8,128)(2,1)} %v_ref.3, bf16[512,256]{1,0:T(8,128)(2,1)} %o_ref.1, ...), custom_call_target="tpu_custom_call" | custom-call | tf_op jit(solution)/shard_map/spread/pallas_call | solution.py:441
  70.3 28.8 %attend.1 = (bf16[4096,128]{1,0:T(8,128)(2,1)}, bf16[2048,128]{1,0:T(8,128)(2,1)}, bf16[2048,128]{1,0:T(8,128)(2,1)}, bf16[512,256]{1,0:T(8,128)(2,1)}, bf16[512...) custom-call(s32[512]{0:T(512)} %sizes.1, bf16[4096,128]{1,0:T(8,128)(2,1)} %get-tuple-element.14.qg, ...), custom_call_target="tpu_custom_call" | custom-call | tf_op jit(solution)/shard_map/attend/pallas_call | solution.py:464
  99.1 62.0 %collect.1 = (bf16[512,256]{1,0:T(8,128)(2,1)}, bf16[512,256]{1,0:T(8,128)(2,1)}, bf16[512,256]{1,0:T(8,128)(2,1)}) custom-call(bf16[4096,128]{1,0:T(8,128)(2,1)} %get-tuple-element.19.dq, bf16[2048,128]{1,0:T(8,128)(2,1)} %get-tuple-element.20.dk, bf16[2048,128]{1,0:T(8,128)(2,1)} %get-tuple-element.21.dv, bf16[512,256]{1,0:T(8,128)(2,1)} %get-tuple-element.22.dq_own, ...), custom_call_target="tpu_custom_call" | custom-call | tf_op jit(solution)/shard_map/collect/pallas_call | solution.py:485
  161.1 1.7 %copy.15 = bf16[512,256]{1,0:T(8,128)(2,1)} copy(bf16[512,256]{1,0:T(8,128)(2,1)} %get-tuple-element.28) | data formatting | bytes 524288
  162.8 1.7 %copy.16 = bf16[512,256]{1,0:T(8,128)(2,1)} copy(bf16[512,256]{1,0:T(8,128)(2,1)} %get-tuple-element.29) | data formatting | bytes 524288
  164.5 1.7 %copy.17 = bf16[512,256]{1,0:T(8,128)(2,1)} copy(bf16[512,256]{1,0:T(8,128)(2,1)} %get-tuple-element.30) | data formatting | bytes 524288

commit v2 on v0

v2 whole, which is shorter than its diff:
```python
import functools
import math

import jax
import jax.numpy as jnp
from jax import lax
from jax.experimental import pallas as pl
from jax.experimental.pallas import tpu as pltpu
from jax.sharding import PartitionSpec as P

HD = 128
UNIT = 32
ROWS = 512
STRIPE = 128
TASK_K = 2048
PEERS = 32
SHARDS = 16
SCALE = HD ** -0.5
MESH = pl.DeviceIdType.MESH
F32 = jnp.float32
BF16 = jnp.bfloat16
CONTRACT = (((1,), (0,)), ((), ()))
CONTRACT_LAST = (((1,), (1,)), ((), ()))
CONTRACT_FIRST = (((0,), (0,)), ((), ()))


def where_am_i():
    seq = lax.axis_index("seq")
    return seq, seq // 8, (seq // 2) % 4, seq % 2


def multiple(value, of):
    return pl.multiple_of(value, of)


def push(here, there, device, me, send_sem, recv_sem):
    seq, head = device

    @pl.when(seq == me)
    def _():
        pltpu.make_async_copy(here, there, recv_sem).start()

    @pl.when(seq != me)
    def _():
        pltpu.make_async_remote_copy(
            src_ref=here, dst_ref=there, send_sem=send_sem, recv_sem=recv_sem,
            device_id=(seq, head), device_id_type=MESH,
        ).start()


def wait_bytes(ref, sem):
    pltpu.make_async_copy(ref, ref, sem).wait()


def dot(a, b, dims):
    return lax.dot_general(a, b, dims, preferred_element_type=F32)


def tile(q, d, keys, values, mask):
    score = dot(jnp.concatenate([q, d[:, HD:]], axis=1), keys, CONTRACT_LAST)
    probs = jnp.exp2(score * (SCALE * math.log2(math.e)))
    if mask is not None:
        probs = jnp.where(mask, probs, 0.0)
    grad = (probs * dot(d, values, CONTRACT_LAST)).astype(BF16)
    dq = dot(grad, keys[:, :HD], CONTRACT)
    dk = dot(grad, q, CONTRACT_FIRST)
    dv = dot(probs.astype(BF16), d[:, :HD], CONTRACT_FIRST)
    return dq, dk, dv


def pick(rows, first, last):
    lane = lax.broadcasted_iota(jnp.int32, (rows, HD), 1)
    return jnp.where((lane >= first) & (lane <= last), -1.0, 0.0).astype(BF16)


def layer_kernel(
    sizes, q_ref, k_ref, v_ref, o_ref, g_ref, w_ref, n_ref,
    dq_out, dk_out, dv_out,
    landed, qg, dg, kg, vg, dl,
    dq_sum, dk_sum, dv_sum, row_block, key_block, own_block, dq_own,
    dq_part, to_sibling, from_sibling, key_part, rq, rk,
    ring_send, ring_recv, q_send, k_send, v_send, d_send, q_recv, k_recv, v_recv, d_recv,
    dq_send, dq_recv, sibling_send, sibling_recv, part_send, part_recv,
):
    me, x, y, core = where_am_i()
    head = lax.axis_index("head")
    right, left = lax.rem(head + 1, 8), lax.rem(head + 7, 8)
    place = me % SHARDS
    clean = me >= SHARDS
    own_slot = x % 2
    own_group = y + own_slot * (3 - 2 * y)
    own_row = (x // 2) * 128 + core * 64
    group = y // 2 * 2 + core
    which = y % 2
    sibling = me + 1 - 2 * core

    barrier = pltpu.get_barrier_semaphore()

    def greet(step, carry):
        pl.semaphore_signal(
            barrier, inc=1, device_id=(lax.rem(me + step, PEERS), head), device_id_type=MESH
        )
        return carry

    lax.fori_loop(1, PEERS, greet, 0)
    for neighbour in (left, right):
        pl.semaphore_signal(barrier, inc=1, device_id=(me, neighbour), device_id_type=MESH)
    pl.semaphore_wait(barrier, PEERS + 1)

    def ring(direction, index, source):
        return pltpu.make_async_remote_copy(
            src_ref=source,
            dst_ref=landed.at[index, direction],
            send_sem=ring_send.at[direction, index],
            recv_sem=ring_recv.at[direction, index],
            device_id=(me, (right, left)[direction]),
            device_id_type=MESH,
        )

    for index in range(2):
        for direction in range(2):
            unit = index if direction == 0 else 1 - index
            ring(direction, index, g_ref.at[pl.ds(unit * UNIT, UNIT)]).start()

    def task_of(index):
        stripe, part = index // 2, index % 2
        return (stripe * 4 + own_group // 2 * 2 + part) * 2 + own_group % 2

    def send_queries(step, carry):
        index = lax.rem(me + step, 8)
        column = multiple(index % 2 * HD, HD)
        push(
            q_ref.at[:, :, pl.ds(column, HD)],
            qg.at[own_slot, :, pl.ds(multiple(own_row, 64), 64)],
            (task_of(index), head), me, q_send.at[index], q_recv,
        )
        return carry

    lax.fori_loop(0, 8, send_queries, 0)

    @pl.when(clean)
    def _():
        def send_keys(step, carry):
            device = lax.rem(me + step, PEERS)
            row = multiple(device // 8 * STRIPE, STRIPE)
            column = multiple(device // 2 % 2 * HD, HD)
            target = pl.ds(multiple(place * STRIPE, STRIPE), STRIPE)
            for source, there, send, recv in ((k_ref, kg, k_send, k_recv), (v_ref, vg, v_send, v_recv)):
                push(
                    source.at[pl.ds(row, STRIPE), pl.ds(column, HD)],
                    there.at[target, pl.ds(0, HD)],
                    (device, head), me, send.at[device], recv,
                )
            return carry

        lax.fori_loop(0, PEERS, send_keys, 0)

    lane = lax.broadcasted_iota(jnp.int32, (UNIT, HD), 1)

    def produce(grad, start):
        rows = pl.ds(multiple(start, UNIT), UNIT)
        norms = n_ref[rows, :].astype(F32) * (1.0 / SCALE)
        for h in range(2):
            columns = slice(h * HD, (h + 1) * HD)
            part = grad[:, columns]
            delta = jnp.sum(
                part.astype(F32) * o_ref[rows, columns].astype(F32), axis=1, keepdims=True
            ).astype(BF16).astype(F32)
            norm = norms[:, h:h + 1]
            high = norm.astype(BF16).astype(F32)
            rest = norm - high
            middle = rest.astype(BF16).astype(F32)
            low = rest - middle
            extra = jnp.where(lane == 0, high, 0.0)
            extra = jnp.where(lane == 1, middle, extra)
            extra = jnp.where(lane == 2, low, extra)
            extra = jnp.where(lane == 3, delta, extra)
            dl[rows, h * 256:h * 256 + HD] = part
            dl[rows, h * 256 + HD:(h + 1) * 256] = extra.astype(BF16)

    def project(rows):
        return dot(rows, w_ref[...], CONTRACT_LAST).astype(BF16)

    def send_grads(chunk):
        def send(step, carry):
            index = lax.rem(me + step, 8)
            column = multiple(index % 2 * 256, 256)
            push(
                dl.at[pl.ds(multiple(chunk * 64, 64), 64), pl.ds(column, 256)],
                dg.at[own_slot, chunk, pl.ds(multiple(own_row, 64), 64)],
                (task_of(index), head), me, d_send.at[index], d_recv.at[chunk],
            )
            return carry

        lax.fori_loop(0, 8, send, 0)

    grad = project(g_ref[...])
    for unit in range(2):
        produce(grad[unit * UNIT:(unit + 1) * UNIT], head * 64 + unit * UNIT)
    send_grads(head)

    kg[:, HD:] = pick(TASK_K, 0, 2)
    vg[:, HD:] = pick(TASK_K, 3, 3)
    dk_sum[...] = jnp.zeros_like(dk_sum)
    dv_sum[...] = jnp.zeros_like(dv_sum)
    in_group = lax.broadcasted_iota(jnp.int32, (32, HD), 0)

    def coarse_of(slot):
        return group + slot * (7 - 2 * group)

    def number_rows(index, carry):
        slot, chunk, half, pair = index // 32, index // 4 % 8, index // 2 % 2, index % 2
        pair = coarse_of(slot) * 32 + half * 16 + chunk * 2 + pair
        block = 2 * pair + jnp.where(in_group >= sizes[2 * pair], 1, 0)
        row = half * 64 + index % 2 * 32
        row_block[slot, chunk, pl.ds(multiple(row, 32), 32), :] = block
        row_block[slot, chunk, pl.ds(multiple(128 + row, 32), 32), :] = block + 1
        return carry

    lax.fori_loop(0, 64, number_rows, 0)
    row_lane = lax.broadcasted_iota(jnp.int32, (1, HD), 1)

    def number_keys(index, carry):
        blocks = []
        for half in range(2):
            pair = (index * 1024 + half * ROWS + x * STRIPE) // 32
            part = row_lane // 32
            size = jnp.where(
                part < 2,
                jnp.where(part == 0, sizes[2 * pair], sizes[2 * pair + 2]),
                jnp.where(part == 2, sizes[2 * pair + 4], sizes[2 * pair + 6]),
            )
            blocks.append(2 * (pair + part) + jnp.where(row_lane % 32 >= size, 1, 0))
        key_block[index] = jnp.concatenate(blocks, axis=1)
        return carry

    lax.fori_loop(0, 8, number_keys, 0)

    def query_owner(index):
        slot, kind, half = index // 4, index // 2 % 2, index % 2
        return kind * SHARDS + 2 * coarse_of(slot) + half

    def attend(turn, carry):
        chunk = lax.rem(head + 8 + (turn + 1) // 2 * (1 - 2 * (turn % 2)), 8)

        @pl.when(turn == 0)
        def _():
            wait_bytes(qg, q_recv)
            wait_bytes(kg.at[:, pl.ds(0, HD)], k_recv)
            wait_bytes(vg.at[:, pl.ds(0, HD)], v_recv)

        wait_bytes(dg.at[:, chunk], d_recv.at[chunk])
        dq_sum[...] = jnp.zeros_like(dq_sum)
        later = None
        for number in range(9):
            slot = 1 if number >= 4 else (number - group + 3) // 4
            pair = number - slot * (group + 1)
            keys = pl.ds(multiple(pair * 256, 256), 256)
            mask = None
            if number < 4 or number == 8:
                own = row_block[slot, chunk]
                mask = jnp.concatenate([own, own], axis=1) > key_block[pair]
            dq, dk, dv = tile(qg[slot, chunk], dg[slot, chunk], kg[keys, :], vg[keys, :], mask)
            dk_sum[keys, :] += dk
            dv_sum[keys, :] += dv
            if number < 4:
                dq_sum[slot] += dq
            else:
                later = dq if later is None else later + dq
        first = (dq_sum[0] * SCALE).astype(BF16)
        second = ((dq_sum[1] + later) * SCALE).astype(BF16)
        for index in range(8):
            part = (first, second)[index // 4]
            dq_part[chunk, index] = part[index % 4 * 64:(index % 4 + 1) * 64]

        def send(step, inner):
            index = lax.rem(me + step, 8)
            push(
                dq_part.at[chunk, index],
                rq.at[x, chunk, :, pl.ds(multiple(which * HD, HD), HD)],
                (query_owner(index), head), me, dq_send.at[index], dq_recv,
            )
            return inner

        lax.fori_loop(0, 8, send, 0)
        return carry

    def attended(step):
        return step - (step + 7) // 8 + step // 6 + step // 7

    def step(index, carry):
        for direction in range(2):
            ring(direction, index, landed.at[index, direction]).wait_recv()

            @pl.when(index < 5)
            def _():
                ring(direction, lax.rem(index + 2, 7), landed.at[index, direction]).start()

        away = index // 2 + 1
        chunks = (lax.rem(head + 8 - away, 8), lax.rem(head + away, 8))
        units = (index % 2, 1 - index % 2)
        grad = project(landed[index].reshape(2 * UNIT, 4096))
        for direction in range(2):
            produce(
                grad[direction * UNIT:(direction + 1) * UNIT],
                chunks[direction] * 64 + units[direction] * UNIT,
            )

        @pl.when(index % 2 == 1)
        def _():
            send_grads(chunks[0])

        @pl.when((index % 2 == 1) | (index == 6))
        def _():
            send_grads(chunks[1])

        lax.fori_loop(attended(index), attended(index + 1), attend, 0)
        return carry

    lax.fori_loop(0, 7, step, 0)

    def narrow(index, carry):
        there = pl.ds(multiple(index * 256 + (1 - core) * STRIPE, STRIPE), STRIPE)
        to_sibling[0, index] = (dk_sum[there, :] * SCALE).astype(BF16)
        to_sibling[1, index] = dv_sum[there, :].astype(BF16)
        return carry

    lax.fori_loop(0, 8, narrow, 0)
    across = pltpu.make_async_remote_copy(
        src_ref=to_sibling, dst_ref=from_sibling, send_sem=sibling_send, recv_sem=sibling_recv,
        device_id=(sibling, head), device_id_type=MESH,
    )
    across.start()
    across.wait_recv()

    def pass_on(step, carry):
        index = lax.rem(me // 2 + step, 8)
        here = pl.ds(multiple(index * 256 + core * STRIPE, STRIPE), STRIPE)
        key_part[index, 0] = (
            dk_sum[here, :] * SCALE + from_sibling[0, index].astype(F32)
        ).astype(BF16)
        key_part[index, 1] = (dv_sum[here, :] + from_sibling[1, index].astype(F32)).astype(BF16)
        push(
            key_part.at[index],
            rk.at[y // 2, :, pl.ds(multiple(x * STRIPE, STRIPE), STRIPE), pl.ds(multiple(which * HD, HD), HD)],
            (SHARDS + 2 * index + core, head), me, part_send.at[index], part_recv,
        )
        return carry

    lax.fori_loop(0, 8, pass_on, 0)

    @pl.when(me < SHARDS)
    def _():
        def number_own(index, carry):
            pair = place * 16 + index
            own_block[pl.ds(multiple(index * 32, 32), 32), :] = 2 * pair + jnp.where(
                in_group >= sizes[2 * pair], 1, 0
            )
            return carry

        lax.fori_loop(0, 16, number_own, 0)
        for part in range(4):
            rows = slice(part * STRIPE, (part + 1) * STRIPE)
            block = own_block[rows, :].astype(F32)
            mask = block == block.T
            for h in range(2):
                columns = slice(h * HD, (h + 1) * HD)
                dq, dk, dv = tile(
                    q_ref[2 * part:2 * part + 2, :, columns].reshape(STRIPE, HD),
                    dl[rows, h * 256:(h + 1) * 256],
                    jnp.concatenate([k_ref[rows, columns], pick(STRIPE, 0, 2)], axis=1),
                    jnp.concatenate([v_ref[rows, columns], pick(STRIPE, 3, 3)], axis=1),
                    mask,
                )
                dq_own[rows, columns] = dq * SCALE
                dk_out[rows, columns] = (dk * SCALE).astype(BF16)
                dv_out[rows, columns] = dv.astype(BF16)

    wait_bytes(rq, dq_recv)

    def summed_queries():
        parts = [rq[stripe].reshape(ROWS, 256).astype(F32) for stripe in range(4)]
        return (parts[0] + parts[1]) + (parts[2] + parts[3])

    @pl.when(me < SHARDS)
    def _():
        dq_out[...] = (summed_queries() + dq_own[...]).astype(BF16)

    @pl.when(clean)
    def _():
        dq_out[...] = summed_queries().astype(BF16)
        wait_bytes(rk, part_recv)
        dk_out[...] = (rk[0, 0].astype(F32) + rk[1, 0].astype(F32)).astype(BF16)
        dv_out[...] = (rk[0, 1].astype(F32) + rk[1, 1].astype(F32)).astype(BF16)

    for index in range(7):
        for direction in range(2):
            ring(direction, index, landed.at[index, direction]).wait_send()
    across.wait_send()

    def settle(index, carry):
        @pl.when(task_of(index) != me)
        def _():
            wait_bytes(q_ref.at[:, :, pl.ds(0, HD)], q_send.at[index])
            wait_bytes(dl.at[:, pl.ds(0, 256)], d_send.at[index])

        @pl.when(query_owner(index) != me)
        def _():
            wait_bytes(dq_part.at[:, index], dq_send.at[index])

        @pl.when(SHARDS + 2 * index + core != me)
        def _():
            wait_bytes(key_part.at[index], part_send.at[index])
        return carry

    lax.fori_loop(0, 8, settle, 0)

    @pl.when(clean)
    def _():
        def settle_keys(step, carry):
            device = lax.rem(me + step, PEERS)
            wait_bytes(k_ref.at[pl.ds(0, STRIPE), pl.ds(0, HD)], k_send.at[device])
            wait_bytes(v_ref.at[pl.ds(0, STRIPE), pl.ds(0, HD)], v_send.at[device])
            return carry

        lax.fori_loop(1, PEERS, settle_keys, 0)


VMEM = pl.BlockSpec(memory_space=pltpu.VMEM)
SMEM = pl.BlockSpec(memory_space=pltpu.SMEM)
DMA = pltpu.SemaphoreType.DMA
LIMIT = 56 * 1024 * 1024


def shards(queries, keys, values, attn_out, out_grad, out_weight, log_norm, block_sizes):
    return pl.pallas_call(
        layer_kernel,
        name="layer",
        out_shape=(jax.ShapeDtypeStruct((ROWS, 256), BF16),) * 3,
        in_specs=[SMEM] + [VMEM] * 7,
        out_specs=(VMEM,) * 3,
        scratch_shapes=[
            pltpu.VMEM((7, 2, UNIT, 4096), BF16),
            pltpu.VMEM((2, 8, 256, HD), BF16),
            pltpu.VMEM((2, 8, 256, 256), BF16),
            pltpu.VMEM((TASK_K, 256), BF16),
            pltpu.VMEM((TASK_K, 256), BF16),
            pltpu.VMEM((ROWS, 512), BF16),
            pltpu.VMEM((2, 256, HD), F32),
            pltpu.VMEM((TASK_K, HD), F32),
            pltpu.VMEM((TASK_K, HD), F32),
            pltpu.VMEM((2, 8, 256, HD), jnp.int32),
            pltpu.VMEM((8, 1, 256), jnp.int32),
            pltpu.VMEM((ROWS, HD), jnp.int32),
            pltpu.VMEM((ROWS, 256), F32),
            pltpu.VMEM((8, 8, 64, HD), BF16),
            pltpu.VMEM((2, 8, STRIPE, HD), BF16),
            pltpu.VMEM((2, 8, STRIPE, HD), BF16),
            pltpu.VMEM((8, 2, STRIPE, HD), BF16),
            pltpu.VMEM((4, 8, 64, 256), BF16),
            pltpu.VMEM((2, 2, ROWS, 256), BF16),
            DMA((2, 7)), DMA((2, 7)), DMA((8,)), DMA((PEERS,)), DMA((PEERS,)), DMA((8,)),
            DMA, DMA, DMA, DMA((8,)),
            DMA((8,)), DMA, DMA, DMA, DMA((8,)), DMA,
        ],
        compiler_params=pltpu.CompilerParams(
            collective_id=0, has_side_effects=True, vmem_limit_bytes=LIMIT
        ),
    )(
        block_sizes, queries.reshape(8, 64, 256), keys, values, attn_out, out_grad, out_weight,
        log_norm,
    )


def solution(mesh):
    in_specs = (
        P("seq", "head"),
        P("seq", "head"),
        P("seq", "head"),
        P("seq", "head"),
        P(("seq", "head"), None),
        P("head", None),
        P("seq", "head"),
        P(),
    )
    out_specs = (P("seq", "head"), P("seq", "head"), P("seq", "head"))
    return jax.shard_map(shards, mesh=mesh, in_specs=in_specs, out_specs=out_specs, check_vma=False)
```

time: 679 us -> 124 us (0.18)
  waiting for transfers between devices: 314 us -> 0 us
  local copies, waits for them, and re-layouts: 143 us -> 6.5 us
  Pallas kernels: 0 us -> 117 us
  other arithmetic: 98 us -> 0 us
  blocking collectives: 46.3 us -> 0 us
  matrix products: 45.6 us -> 0 us
  between operations: 13.8 us -> 0.64 us
  loops' own time: 12.3 us -> 0 us
    reduce_scatter x1 -> x0, waiting for transfers between devices: 175 us -> none  [shards(): lax.psum_scatter(folded[-1].astype(jnp.bfloat16), 'seq', scatter_dimensio...]
    all_gather x3 -> x0, waiting for transfers between devices: 139 us -> none  [the longest x1 67.4 us: shards(): grad_piece = lax.all_gather(head_grad, 'seq', axis=0, tiled=True)]
    pallas_call x0 -> x1, Pallas kernels: none -> 117 us  [shards(): pl.pallas_call(layer_kernel, name='layer', out_shape=(jax.ShapeDtypeStruc...]
    dynamic_slice x48 -> x0, local copies, waits for them, and re-layouts: 79.1 us -> none  [the longest x32 61.3 us: one_block(): current = lax.dynamic_slice_in_dim(updated[-1], offset, unit, 0)]
    reduce_or x16 -> x0, other arithmetic: 46.7 us -> none  [one_block(): jnp.any(mask)]
    all_gather x2 -> x0, blocking collectives: 46.3 us -> none  [the longest x1 24.4 us: shards(): norm_piece = lax.all_gather(log_norm, 'seq', axis=0, tiled=True)]
    dot_general x41 -> x0, matrix products: 45.6 us -> none  [the longest x8 15.9 us: tile_grads(): jnp.einsum('qhd,khd->hqk', grad_three, value_three, preferred_element_typ...]
    dynamic_update_slice x32 -> x0, local copies, waits for them, and re-layouts: 41.9 us -> none  [one_block(): lax.dynamic_update_slice_in_dim(updated[-1], current + query_total, offse...]
  transfers between devices with their start and end apart: 4 -> 0, of which waited for: 4 -> 0; matrix products, arithmetic and copies ran while one was open for 2% -> 0% of each run, Pallas kernels for 0% -> 0%
where the time goes in v2:
time: 124 us
  Pallas kernels  117 us (94%)
  local copies, waits for them, and re-layouts  6.5 us (5%)
    pallas_call x1, Pallas kernels, shards(): pl.pallas_call(layer_kernel, name='layer', out_shape=(jax.ShapeDtypeStruc...  117 us
    unnamed x4, local copies, waits for them, and re-layouts  6.5 us

profile of v2, /device:TPU:7, one launch (start us, length us, event | category | flops | bytes accessed | tf_op | source)
XLA Modules:
  0.0 123.9 jit_solution(13826236467355092713)
XLA Ops:
  0.6 1.5 %copy.11.n_ref = bf16[512,2]{1,0:T(8,128)(2,1)} copy(bf16[512,2]{0,1:T(2,128)(2,1)} %param.14) | data formatting | bytes 4096 | tf_op args[6]
  2.1 116.7 %layer.1 = (bf16[512,256]{1,0:T(8,128)(2,1)}, bf16[512,256]{1,0:T(8,128)(2,1)}, bf16[512,256]{1,0:T(8,128)(2,1)}) custom-call(s32[512]{0:T(512)} %sizes.1, bf16[8,64,256]{2,1,0:T(8,128)(2,1)} %bitcast.1, bf16[512,256]{1,0:T(8,128)(2,1)} %k_ref.1, bf16[512,256]{1,0:T(8,128)(2,1)} %v_ref.1, bf16[512,256]{1,0:T(8,128)(2,1)} %o_ref.1, bf16[64,4096]{1,0:T(8,128)(2,1)} %g_ref.1, ...), custom_call_target="tpu_custom_call" | custom-call | tf_op jit(solution)/shard_map/layer/pallas_call | solution.py:436
  118.8 1.7 %copy.15 = bf16[512,256]{1,0:T(8,128)(2,1)} copy(bf16[512,256]{1,0:T(8,128)(2,1)} %get-tuple-element.6) | data formatting | bytes 524288
  120.5 1.7 %copy.16 = bf16[512,256]{1,0:T(8,128)(2,1)} copy(bf16[512,256]{1,0:T(8,128)(2,1)} %get-tuple-element.7) | data formatting | bytes 524288
  122.2 1.7 %copy.17 = bf16[512,256]{1,0:T(8,128)(2,1)} copy(bf16[512,256]{1,0:T(8,128)(2,1)} %get-tuple-element.8) | data formatting | bytes 524288

commit v3 on v2

--- a/solution.py
+++ b/solution.py
@@ -10,11 +10,13 @@
 
 HD = 128
 UNIT = 32
+SIDE = 16
 ROWS = 512
 STRIPE = 128
 TASK_K = 2048
 PEERS = 32
 SHARDS = 16
+CHIPS = 16
 SCALE = HD ** -0.5
 MESH = pl.DeviceIdType.MESH
 F32 = jnp.float32
@@ -56,31 +58,42 @@
     return lax.dot_general(a, b, dims, preferred_element_type=F32)
 
 
-def tile(q, d, keys, values, mask):
-    score = dot(jnp.concatenate([q, d[:, HD:]], axis=1), keys, CONTRACT_LAST)
+def tile(q, d, extra, keys, values, mask):
+    score = dot(jnp.concatenate([q, extra], axis=1), keys, CONTRACT_LAST)
     probs = jnp.exp2(score * (SCALE * math.log2(math.e)))
     if mask is not None:
         probs = jnp.where(mask, probs, 0.0)
-    grad = (probs * dot(d, values, CONTRACT_LAST)).astype(BF16)
+    grad = (probs * dot(jnp.concatenate([d, extra], axis=1), values, CONTRACT_LAST)).astype(BF16)
     dq = dot(grad, keys[:, :HD], CONTRACT)
     dk = dot(grad, q, CONTRACT_FIRST)
-    dv = dot(probs.astype(BF16), d[:, :HD], CONTRACT_FIRST)
+    dv = dot(probs.astype(BF16), d, CONTRACT_FIRST)
     return dq, dk, dv
 
 
 def pick(rows, first, last):
     lane = lax.broadcasted_iota(jnp.int32, (rows, HD), 1)
-    return jnp.where((lane >= first) & (lane <= last), -1.0, 0.0).astype(BF16)
+    part = lane % SIDE
+    return jnp.where((lane < 4 * SIDE) & (part >= first) & (part <= last), -1.0, 0.0).astype(BF16)
+
+
+def side(pieces):
+    stacked = jnp.concatenate([piece.astype(F32) for piece in pieces], axis=0)
+    filler = jnp.zeros((HD - stacked.shape[0], HD), F32)
+    turned = jnp.concatenate([stacked, filler], axis=0).T[:64]
+    lane = lax.broadcasted_iota(jnp.int32, (64, HD), 1)
+    return jnp.concatenate(
+        [jnp.where(lane // SIDE == number, turned, 0.0) for number in range(len(pieces))], axis=0
+    ).astype(BF16)
 
 
 def layer_kernel(
     sizes, q_ref, k_ref, v_ref, o_ref, g_ref, w_ref, n_ref,
     dq_out, dk_out, dv_out,
-    landed, qg, dg, kg, vg, dl,
+    landed, qg, dg, kg, vg, dl, norms, extras,
     dq_sum, dk_sum, dv_sum, row_block, key_block, own_block, dq_own,
     dq_part, to_sibling, from_sibling, key_part, rq, rk,
     ring_send, ring_recv, q_send, k_send, v_send, d_send, q_recv, k_recv, v_recv, d_recv,
-    dq_send, dq_recv, sibling_send, sibling_recv, part_send, part_recv,
+    dq_send, dq_recv, sibling_send, sibling_recv, part_send, part_recv, relay_send,
 ):
     me, x, y, core = where_am_i()
     head = lax.axis_index("head")
@@ -89,9 +102,9 @@
     clean = me >= SHARDS
     own_slot = x % 2
     own_group = y + own_slot * (3 - 2 * y)
-    own_row = (x // 2) * 128 + core * 64
-    group = y // 2 * 2 + core
-    which = y % 2
+    own_piece = (x // 2) * 2 + core
+    group = core * 2 + y % 2
+    which = y // 2
     sibling = me + 1 - 2 * core
 
     barrier = pltpu.get_barrier_semaphore()
@@ -124,14 +137,14 @@
 
     def task_of(index):
         stripe, part = index // 2, index % 2
-        return (stripe * 4 + own_group // 2 * 2 + part) * 2 + own_group % 2
+        return (stripe * 4 + 2 * part + own_group % 2) * 2 + own_group // 2
 
     def send_queries(step, carry):
         index = lax.rem(me + step, 8)
         column = multiple(index % 2 * HD, HD)
         push(
             q_ref.at[:, :, pl.ds(column, HD)],
-            qg.at[own_slot, :, pl.ds(multiple(own_row, 64), 64)],
+            qg.at[own_slot, :, pl.ds(multiple(own_piece * 64, 64), 64)],
             (task_of(index), head), me, q_send.at[index], q_recv,
         )
         return carry
@@ -141,53 +154,53 @@
     @pl.when(clean)
     def _():
         def send_keys(step, carry):
-            device = lax.rem(me + step, PEERS)
-            row = multiple(device // 8 * STRIPE, STRIPE)
-            column = multiple(device // 2 % 2 * HD, HD)
+            chip = lax.rem(me // 2 + step, CHIPS)
+            row = multiple(chip // 4 * STRIPE, STRIPE)
+            column = multiple(chip // 2 % 2 * HD, HD)
             target = pl.ds(multiple(place * STRIPE, STRIPE), STRIPE)
-            for source, there, send, recv in ((k_ref, kg, k_send, k_recv), (v_ref, vg, v_send, v_recv)):
+            for kind, (source, there, send, recv) in enumerate(
+                ((k_ref, kg, k_send, k_recv), (v_ref, vg, v_send, v_recv))
+            ):
                 push(
                     source.at[pl.ds(row, STRIPE), pl.ds(column, HD)],
                     there.at[target, pl.ds(0, HD)],
-                    (device, head), me, send.at[device], recv,
+                    (2 * chip + kind, head), me, send.at[chip], recv,
                 )
             return carry
 
-        lax.fori_loop(0, PEERS, send_keys, 0)
-
-    lane = lax.broadcasted_iota(jnp.int32, (UNIT, HD), 1)
-
-    def produce(grad, start):
-        rows = pl.ds(multiple(start, UNIT), UNIT)
-        norms = n_ref[rows, :].astype(F32) * (1.0 / SCALE)
-        for h in range(2):
-            columns = slice(h * HD, (h + 1) * HD)
-            part = grad[:, columns]
-            delta = jnp.sum(
-                part.astype(F32) * o_ref[rows, columns].astype(F32), axis=1, keepdims=True
-            ).astype(BF16).astype(F32)
-            norm = norms[:, h:h + 1]
-            high = norm.astype(BF16).astype(F32)
-            rest = norm - high
-            middle = rest.astype(BF16).astype(F32)
-            low = rest - middle
-            extra = jnp.where(lane == 0, high, 0.0)
-            extra = jnp.where(lane == 1, middle, extra)
-            extra = jnp.where(lane == 2, low, extra)
-            extra = jnp.where(lane == 3, delta, extra)
-            dl[rows, h * 256:h * 256 + HD] = part
-            dl[rows, h * 256 + HD:(h + 1) * 256] = extra.astype(BF16)
+        lax.fori_loop(0, CHIPS, send_keys, 0)
 
     def project(rows):
         return dot(rows, w_ref[...], CONTRACT_LAST).astype(BF16)
 
-    def send_grads(chunk):
+    part_row = lax.broadcasted_iota(jnp.int32, (SIDE, 64), 0)
+    norm = n_ref[...].astype(F32) * (1.0 / SCALE)
+    high = norm.astype(BF16).astype(F32)
+    middle = (norm - high).astype(BF16).astype(F32)
+    low = norm - high - middle
+    for chunk in range(8):
+        for h in range(2):
+            cut = (slice(h, h + 1), slice(chunk * 64, (chunk + 1) * 64))
+            rows = jnp.where(part_row == 0, high[cut], 0.0)
+            rows = jnp.where(part_row == 1, middle[cut], rows)
+            rows = jnp.where(part_row == 2, low[cut], rows)
+            norms[chunk, h, :, 0:64] = rows
+
+    def finish(chunk):
+        rows = pl.ds(multiple(chunk * 64, 64), 64)
+        for h in range(2):
+            product = dl[chunk, h, 0:64, :].astype(F32) * o_ref[rows, h * HD:(h + 1) * HD].astype(F32)
+            delta = jnp.sum(product.T, axis=0, keepdims=True).astype(BF16).astype(F32)
+            extra = jnp.where(part_row == 3, delta, norms[chunk, h, :, 0:64])
+            dl[chunk, h, 64:80, :] = jnp.concatenate(
+                [extra, jnp.zeros((SIDE, 64), F32)], axis=1
+            ).astype(BF16)
+
         def send(step, carry):
             index = lax.rem(me + step, 8)
-            column = multiple(index % 2 * 256, 256)
             push(
-                dl.at[pl.ds(multiple(chunk * 64, 64), 64), pl.ds(column, 256)],
-                dg.at[own_slot, chunk, pl.ds(multiple(own_row, 64), 64)],
+                dl.at[chunk, index % 2],
+                dg.at[own_slot, chunk, own_piece],
                 (task_of(index), head), me, d_send.at[index], d_recv.at[chunk],
             )
             return carry
@@ -195,9 +208,9 @@
         lax.fori_loop(0, 8, send, 0)
 
     grad = project(g_ref[...])
-    for unit in range(2):
-        produce(grad[unit * UNIT:(unit + 1) * UNIT], head * 64 + unit * UNIT)
-    send_grads(head)
+    for h in range(2):
+        dl[head, h, 0:64, :] = grad[:, h * HD:(h + 1) * HD]
+    finish(head)
 
     kg[:, HD:] = pick(TASK_K, 0, 2)
     vg[:, HD:] = pick(TASK_K, 3, 3)
@@ -240,17 +253,33 @@
         slot, kind, half = index // 4, index // 2 % 2, index % 2
         return kind * SHARDS + 2 * coarse_of(slot) + half
 
+    def relay(there, recv):
+        half = there.at[:, pl.ds(0, HD)]
+        return pltpu.make_async_remote_copy(
+            src_ref=half, dst_ref=half, send_sem=relay_send, recv_sem=recv,
+            device_id=(sibling, head), device_id_type=MESH,
+        )
+
     def attend(turn, carry):
         chunk = lax.rem(head + 8 + (turn + 1) // 2 * (1 - 2 * (turn % 2)), 8)
 
         @pl.when(turn == 0)
         def _():
             wait_bytes(qg, q_recv)
-            wait_bytes(kg.at[:, pl.ds(0, HD)], k_recv)
-            wait_bytes(vg.at[:, pl.ds(0, HD)], v_recv)
+            for kind, (there, recv) in enumerate(((kg, k_recv), (vg, v_recv))):
+                @pl.when(core == kind)
+                def _():
+                    wait_bytes(there.at[:, pl.ds(0, HD)], recv)
+                    relay(there, recv).start()
+            for kind, (there, recv) in enumerate(((vg, v_recv), (kg, k_recv))):
+                @pl.when(core == kind)
+                def _():
+                    wait_bytes(there.at[:, pl.ds(0, HD)], recv)
 
         wait_bytes(dg.at[:, chunk], d_recv.at[chunk])
         dq_sum[...] = jnp.zeros_like(dq_sum)
+        for slot in range(2):
+            extras[slot] = side([dg[slot, chunk, piece, 64:80, :] for piece in range(4)])
         later = None
         for number in range(9):
             slot = 1 if number >= 4 else (number - group + 3) // 4
@@ -260,7 +289,8 @@
             if number < 4 or number == 8:
                 own = row_block[slot, chunk]
                 mask = jnp.concatenate([own, own], axis=1) > key_block[pair]
-            dq, dk, dv = tile(qg[slot, chunk], dg[slot, chunk], kg[keys, :], vg[keys, :], mask)
+            grads = dg[slot, chunk, :, 0:64, :].reshape(256, HD)
+            dq, dk, dv = tile(qg[slot, chunk], grads, extras[slot], kg[keys, :], vg[keys, :], mask)
             dk_sum[keys, :] += dk
             dv_sum[keys, :] += dv
             if number < 4:
@@ -286,7 +316,7 @@
         return carry
 
     def attended(step):
-        return step - (step + 7) // 8 + step // 6 + step // 7
+        return step // 4 * (2 * step - 7) + step // 7
 
     def step(index, carry):
         for direction in range(2):
@@ -301,18 +331,19 @@
         units = (index % 2, 1 - index % 2)
         grad = project(landed[index].reshape(2 * UNIT, 4096))
         for direction in range(2):
-            produce(
-                grad[direction * UNIT:(direction + 1) * UNIT],
-                chunks[direction] * 64 + units[direction] * UNIT,
-            )
+            rows = pl.ds(multiple(units[direction] * UNIT, UNIT), UNIT)
+            for h in range(2):
+                dl[chunks[direction], h, rows, :] = grad[
+                    direction * UNIT:(direction + 1) * UNIT, h * HD:(h + 1) * HD
+                ]
 
         @pl.when(index % 2 == 1)
         def _():
-            send_grads(chunks[0])
+            finish(chunks[0])
 
         @pl.when((index % 2 == 1) | (index == 6))
         def _():
-            send_grads(chunks[1])
+            finish(chunks[1])
 
         lax.fori_loop(attended(index), attended(index + 1), attend, 0)
         return carry
@@ -342,7 +373,7 @@
         key_part[index, 1] = (dv_sum[here, :] + from_sibling[1, index].astype(F32)).astype(BF16)
         push(
             key_part.at[index],
-            rk.at[y // 2, :, pl.ds(multiple(x * STRIPE, STRIPE), STRIPE), pl.ds(multiple(which * HD, HD), HD)],
+            rk.at[y % 2, :, pl.ds(multiple(x * STRIPE, STRIPE), STRIPE), pl.ds(multiple(which * HD, HD), HD)],
             (SHARDS + 2 * index + core, head), me, part_send.at[index], part_recv,
         )
         return carry
@@ -367,7 +398,8 @@
                 columns = slice(h * HD, (h + 1) * HD)
                 dq, dk, dv = tile(
                     q_ref[2 * part:2 * part + 2, :, columns].reshape(STRIPE, HD),
-                    dl[rows, h * 256:(h + 1) * 256],
+                    dl[2 * part:2 * part + 2, h, 0:64, :].reshape(STRIPE, HD),
+                    side([dl[2 * part + number, h, 64:80, :] for number in range(2)]),
                     jnp.concatenate([k_ref[rows, columns], pick(STRIPE, 0, 2)], axis=1),
                     jnp.concatenate([v_ref[rows, columns], pick(STRIPE, 3, 3)], axis=1),
                     mask,
@@ -397,12 +429,13 @@
         for direction in range(2):
             ring(direction, index, landed.at[index, direction]).wait_send()
     across.wait_send()
+    relay(kg, k_recv).wait_send()
 
     def settle(index, carry):
         @pl.when(task_of(index) != me)
         def _():
             wait_bytes(q_ref.at[:, :, pl.ds(0, HD)], q_send.at[index])
-            wait_bytes(dl.at[:, pl.ds(0, 256)], d_send.at[index])
+            wait_bytes(dl.at[:, 0], d_send.at[index])
 
         @pl.when(query_owner(index) != me)
         def _():
@@ -417,13 +450,14 @@
 
     @pl.when(clean)
     def _():
-        def settle_keys(step, carry):
-            device = lax.rem(me + step, PEERS)
-            wait_bytes(k_ref.at[pl.ds(0, STRIPE), pl.ds(0, HD)], k_send.at[device])
-            wait_bytes(v_ref.at[pl.ds(0, STRIPE), pl.ds(0, HD)], v_send.at[device])
+        def settle_keys(chip, carry):
+            for kind, (source, send) in enumerate(((k_ref, k_send), (v_ref, v_send))):
+                @pl.when(2 * chip + kind != me)
+                def _():
+                    wait_bytes(source.at[pl.ds(0, STRIPE), pl.ds(0, HD)], send.at[chip])
             return carry
 
-        lax.fori_loop(1, PEERS, settle_keys, 0)
+        lax.fori_loop(0, CHIPS, settle_keys, 0)
 
 
 VMEM = pl.BlockSpec(memory_space=pltpu.VMEM)
@@ -442,10 +476,12 @@
         scratch_shapes=[
             pltpu.VMEM((7, 2, UNIT, 4096), BF16),
             pltpu.VMEM((2, 8, 256, HD), BF16),
-            pltpu.VMEM((2, 8, 256, 256), BF16),
+            pltpu.VMEM((2, 8, 4, 64 + SIDE, HD), BF16),
             pltpu.VMEM((TASK_K, 256), BF16),
             pltpu.VMEM((TASK_K, 256), BF16),
-            pltpu.VMEM((ROWS, 512), BF16),
+            pltpu.VMEM((8, 2, 64 + SIDE, HD), BF16),
+            pltpu.VMEM((8, 2, SIDE, HD), F32),
+            pltpu.VMEM((2, 256, HD), BF16),
             pltpu.VMEM((2, 256, HD), F32),
             pltpu.VMEM((TASK_K, HD), F32),
             pltpu.VMEM((TASK_K, HD), F32),
@@ -459,16 +495,16 @@
             pltpu.VMEM((8, 2, STRIPE, HD), BF16),
             pltpu.VMEM((4, 8, 64, 256), BF16),
             pltpu.VMEM((2, 2, ROWS, 256), BF16),
-            DMA((2, 7)), DMA((2, 7)), DMA((8,)), DMA((PEERS,)), DMA((PEERS,)), DMA((8,)),
+            DMA((2, 7)), DMA((2, 7)), DMA((8,)), DMA((CHIPS,)), DMA((CHIPS,)), DMA((8,)),
             DMA, DMA, DMA, DMA((8,)),
-            DMA((8,)), DMA, DMA, DMA, DMA((8,)), DMA,
+            DMA((8,)), DMA, DMA, DMA, DMA((8,)), DMA, DMA,
         ],
         compiler_params=pltpu.CompilerParams(
             collective_id=0, has_side_effects=True, vmem_limit_bytes=LIMIT
         ),
     )(
         block_sizes, queries.reshape(8, 64, 256), keys, values, attn_out, out_grad, out_weight,
-        log_norm,
+        log_norm.T,
     )
 
 

time: 124 us -> 96.2 us (0.78)
  Pallas kernels: 117 us -> 89.4 us
  local copies, waits for them, and re-layouts: 6.5 us -> 5.01 us
    pallas_call x1, Pallas kernels: 117 us -> 89.4 us  [shards(): pl.pallas_call(layer_kernel, name='layer', out_shape=(jax.ShapeDtypeStruc...]
    unnamed x4 -> x3, local copies, waits for them, and re-layouts: 6.5 us -> 5.01 us
where the time goes in v3:
time: 96.2 us; the launch traced here: 95 us
  Pallas kernels  89.4 us (93%)
  local copies, waits for them, and re-layouts  5.01 us (5%)
    pallas_call x1, Pallas kernels, shards(): pl.pallas_call(layer_kernel, name='layer', out_shape=(jax.ShapeDtypeStruc...  89.4 us
    unnamed x3, local copies, waits for them, and re-layouts  5.01 us

profile of v3, /device:TPU:7, one launch (start us, length us, event | category | flops | bytes accessed | tf_op | source)
XLA Modules:
  0.0 95.0 jit_solution(8599912699896003044)
XLA Ops:
  0.6 89.4 %layer.1 = (bf16[512,256]{1,0:T(8,128)(2,1)}, bf16[512,256]{1,0:T(8,128)(2,1)}, bf16[512,256]{1,0:T(8,128)(2,1)}) custom-call(s32[512]{0:T(512)} %sizes.1, bf16[8,64,256]{2,1,0:T(8,128)(2,1)} %bitcast.2, bf16[512,256]{1,0:T(8,128)(2,1)} %k_ref.1, bf16[512,256]{1,0:T(8,128)(2,1)} %v_ref.1, bf16[512,256]{1,0:T(8,128)(2,1)} %o_ref.1, bf16[64,4096]{1,0:T(8,128)(2,1)} %g_ref.1, ...), custom_call_target="tpu_custom_call" | custom-call | tf_op jit(solution)/shard_map/layer/pallas_call | solution.py:470
  90.0 1.7 %copy.14 = bf16[512,256]{1,0:T(8,128)(2,1)} copy(bf16[512,256]{1,0:T(8,128)(2,1)} %get-tuple-element.6) | data formatting | bytes 524288
  91.7 1.7 %copy.15 = bf16[512,256]{1,0:T(8,128)(2,1)} copy(bf16[512,256]{1,0:T(8,128)(2,1)} %get-tuple-element.7) | data formatting | bytes 524288
  93.4 1.7 %copy.16 = bf16[512,256]{1,0:T(8,128)(2,1)} copy(bf16[512,256]{1,0:T(8,128)(2,1)} %get-tuple-element.8) | data formatting | bytes 524288

commit v4 on v3

--- a/solution.py
+++ b/solution.py
@@ -10,6 +10,7 @@
 
 HD = 128
 UNIT = 32
+HALF_UNIT = 16
 SIDE = 16
 ROWS = 512
 STRIPE = 128
@@ -58,15 +59,15 @@
     return lax.dot_general(a, b, dims, preferred_element_type=F32)
 
 
-def tile(q, d, extra, keys, values, mask):
+def tile(q, d, turned_q, turned_d, extra, keys, values, mask):
     score = dot(jnp.concatenate([q, extra], axis=1), keys, CONTRACT_LAST)
     probs = jnp.exp2(score * (SCALE * math.log2(math.e)))
     if mask is not None:
         probs = jnp.where(mask, probs, 0.0)
     grad = (probs * dot(jnp.concatenate([d, extra], axis=1), values, CONTRACT_LAST)).astype(BF16)
     dq = dot(grad, keys[:, :HD], CONTRACT)
-    dk = dot(grad, q, CONTRACT_FIRST)
-    dv = dot(probs.astype(BF16), d, CONTRACT_FIRST)
+    dk = dot(turned_q, grad, CONTRACT)
+    dv = dot(turned_d, probs.astype(BF16), CONTRACT)
     return dq, dk, dv
 
 
@@ -87,13 +88,14 @@
 
 
 def layer_kernel(
-    sizes, q_ref, k_ref, v_ref, o_ref, g_ref, w_ref, n_ref,
+    sizes, q_ref, k_ref, v_ref, g_hbm, w_hbm, o_ref, n_ref,
     dq_out, dk_out, dv_out,
-    landed, qg, dg, kg, vg, dl, norms, extras,
+    g_ref, w_ref, q_own, k_own, v_own,
+    landed, qg, dg, kg, vg, dl, norms, extras, turned,
     dq_sum, dk_sum, dv_sum, row_block, key_block, own_block, dq_own,
     dq_part, to_sibling, from_sibling, key_part, rq, rk,
     ring_send, ring_recv, q_send, k_send, v_send, d_send, q_recv, k_recv, v_recv, d_recv,
-    dq_send, dq_recv, sibling_send, sibling_recv, part_send, part_recv, relay_send,
+    dq_send, dq_recv, sibling_send, sibling_recv, part_send, part_recv, relay_send, fetch,
 ):
     me, x, y, core = where_am_i()
     head = lax.axis_index("head")
@@ -107,6 +109,15 @@
     which = y // 2
     sibling = me + 1 - 2 * core
 
+    fetches = [
+        pltpu.make_async_copy(source, target, fetch.at[number])
+        for number, (source, target) in enumerate(
+            ((g_hbm, g_ref), (w_hbm, w_ref), (q_ref, q_own), (k_ref, k_own), (v_ref, v_own))
+        )
+    ]
+    for number in range(2):
+        fetches[number].start()
+
     barrier = pltpu.get_barrier_semaphore()
 
     def greet(step, carry):
@@ -120,20 +131,22 @@
         pl.semaphore_signal(barrier, inc=1, device_id=(me, neighbour), device_id_type=MESH)
     pl.semaphore_wait(barrier, PEERS + 1)
 
-    def ring(direction, index, source):
+    def ring(direction, index, sub, source):
+        rows = pl.ds(sub * HALF_UNIT, HALF_UNIT)
         return pltpu.make_async_remote_copy(
-            src_ref=source,
-            dst_ref=landed.at[index, direction],
-            send_sem=ring_send.at[direction, index],
-            recv_sem=ring_recv.at[direction, index],
+            src_ref=source.at[rows],
+            dst_ref=landed.at[index, direction, rows],
+            send_sem=ring_send.at[direction, index, sub],
+            recv_sem=ring_recv.at[direction, index, sub],
             device_id=(me, (right, left)[direction]),
             device_id_type=MESH,
         )
 
     for index in range(2):
-        for direction in range(2):
-            unit = index if direction == 0 else 1 - index
-            ring(direction, index, g_ref.at[pl.ds(unit * UNIT, UNIT)]).start()
+        for sub in range(2):
+            for direction in range(2):
+                unit = index if direction == 0 else 1 - index
+                ring(direction, index, sub, g_hbm.at[pl.ds(unit * UNIT, UNIT)]).start()
 
     def task_of(index):
         stripe, part = index // 2, index % 2
@@ -207,6 +220,10 @@
 
         lax.fori_loop(0, 8, send, 0)
 
+    for number in range(2):
+        fetches[number].wait()
+    for number in range(2, 5):
+        fetches[number].start()
     grad = project(g_ref[...])
     for h in range(2):
         dl[head, h, 0:64, :] = grad[:, h * HD:(h + 1) * HD]
@@ -280,6 +297,8 @@
         dq_sum[...] = jnp.zeros_like(dq_sum)
         for slot in range(2):
             extras[slot] = side([dg[slot, chunk, piece, 64:80, :] for piece in range(4)])
+            turned[slot, 0] = qg[slot, chunk].T
+            turned[slot, 1] = dg[slot, chunk, :, 0:64, :].reshape(256, HD).T
         later = None
         for number in range(9):
             slot = 1 if number >= 4 else (number - group + 3) // 4
@@ -290,9 +309,12 @@
                 own = row_block[slot, chunk]
                 mask = jnp.concatenate([own, own], axis=1) > key_block[pair]
             grads = dg[slot, chunk, :, 0:64, :].reshape(256, HD)
-            dq, dk, dv = tile(qg[slot, chunk], grads, extras[slot], kg[keys, :], vg[keys, :], mask)
-            dk_sum[keys, :] += dk
-            dv_sum[keys, :] += dv
+            dq, dk, dv = tile(
+                qg[slot, chunk], grads, turned[slot, 0], turned[slot, 1], extras[slot],
+                kg[keys, :], vg[keys, :], mask,
+            )
+            dk_sum[pair] += dk
+            dv_sum[pair] += dv
             if number < 4:
                 dq_sum[slot] += dq
             else:
@@ -319,12 +341,14 @@
         return step // 4 * (2 * step - 7) + step // 7
 
     def step(index, carry):
-        for direction in range(2):
-            ring(direction, index, landed.at[index, direction]).wait_recv()
-
-            @pl.when(index < 5)
-            def _():
-                ring(direction, lax.rem(index + 2, 7), landed.at[index, direction]).start()
+        for sub in range(2):
+            for direction in range(2):
+                source = landed.at[index, direction]
+                ring(direction, index, sub, source).wait_recv()
+
+                @pl.when(index < 5)
+                def _():
+                    ring(direction, lax.rem(index + 2, 7), sub, source).start()
 
         away = index // 2 + 1
         chunks = (lax.rem(head + 8 - away, 8), lax.rem(head + away, 8))
@@ -351,9 +375,9 @@
     lax.fori_loop(0, 7, step, 0)
 
     def narrow(index, carry):
-        there = pl.ds(multiple(index * 256 + (1 - core) * STRIPE, STRIPE), STRIPE)
-        to_sibling[0, index] = (dk_sum[there, :] * SCALE).astype(BF16)
-        to_sibling[1, index] = dv_sum[there, :].astype(BF16)
+        there = pl.ds(multiple((1 - core) * STRIPE, STRIPE), STRIPE)
+        to_sibling[0, index] = (dk_sum[index, :, there] * SCALE).T.astype(BF16)
+        to_sibling[1, index] = dv_sum[index, :, there].T.astype(BF16)
         return carry
 
     lax.fori_loop(0, 8, narrow, 0)
@@ -366,11 +390,13 @@
 
     def pass_on(step, carry):
         index = lax.rem(me // 2 + step, 8)
-        here = pl.ds(multiple(index * 256 + core * STRIPE, STRIPE), STRIPE)
+        here = pl.ds(multiple(core * STRIPE, STRIPE), STRIPE)
         key_part[index, 0] = (
-            dk_sum[here, :] * SCALE + from_sibling[0, index].astype(F32)
+            (dk_sum[index, :, here] * SCALE).T + from_sibling[0, index].astype(F32)
         ).astype(BF16)
-        key_part[index, 1] = (dv_sum[here, :] + from_sibling[1, index].astype(F32)).astype(BF16)
+        key_part[index, 1] = (
+            dv_sum[index, :, here].T + from_sibling[1, index].astype(F32)
+        ).astype(BF16)
         push(
             key_part.at[index],
             rk.at[y % 2, :, pl.ds(multiple(x * STRIPE, STRIPE), STRIPE), pl.ds(multiple(which * HD, HD), HD)],
@@ -379,6 +405,9 @@
         return carry
 
     lax.fori_loop(0, 8, pass_on, 0)
+
+    for number in range(2, 5):
+        fetches[number].wait()
 
     @pl.when(me < SHARDS)
     def _():
@@ -396,17 +425,18 @@
             mask = block == block.T
             for h in range(2):
                 columns = slice(h * HD, (h + 1) * HD)
+                own_q = q_own[2 * part:2 * part + 2, :, columns].reshape(STRIPE, HD)
+                own_d = dl[2 * part:2 * part + 2, h, 0:64, :].reshape(STRIPE, HD)
                 dq, dk, dv = tile(
-                    q_ref[2 * part:2 * part + 2, :, columns].reshape(STRIPE, HD),
-                    dl[2 * part:2 * part + 2, h, 0:64, :].reshape(STRIPE, HD),
+                    own_q, own_d, own_q.T, own_d.T,
                     side([dl[2 * part + number, h, 64:80, :] for number in range(2)]),
-                    jnp.concatenate([k_ref[rows, columns], pick(STRIPE, 0, 2)], axis=1),
-                    jnp.concatenate([v_ref[rows, columns], pick(STRIPE, 3, 3)], axis=1),
+                    jnp.concatenate([k_own[rows, columns], pick(STRIPE, 0, 2)], axis=1),
+                    jnp.concatenate([v_own[rows, columns], pick(STRIPE, 3, 3)], axis=1),
                     mask,
                 )
                 dq_own[rows, columns] = dq * SCALE
-                dk_out[rows, columns] = (dk * SCALE).astype(BF16)
-                dv_out[rows, columns] = dv.astype(BF16)
+                dk_out[rows, columns] = (dk * SCALE).T.astype(BF16)
+                dv_out[rows, columns] = dv.T.astype(BF16)
 
     wait_bytes(rq, dq_recv)
 
@@ -427,7 +457,8 @@
 
     for index in range(7):
         for direction in range(2):
-            ring(direction, index, landed.at[index, direction]).wait_send()
+            for sub in range(2):
+                ring(direction, index, sub, landed.at[index, direction]).wait_send()
     across.wait_send()
     relay(kg, k_recv).wait_send()
 
@@ -460,20 +491,42 @@
         lax.fori_loop(0, CHIPS, settle_keys, 0)
 
 
+ANY = pl.BlockSpec(memory_space=pl.ANY)
 VMEM = pl.BlockSpec(memory_space=pltpu.VMEM)
 SMEM = pl.BlockSpec(memory_space=pltpu.SMEM)
 DMA = pltpu.SemaphoreType.DMA
 LIMIT = 56 * 1024 * 1024
 
 
+def hand_on_kernel(*refs):
+    for source, target in zip(refs[:3], refs[3:]):
+        target[...] = source[...]
+
+
+def hand_on(results):
+    return pl.pallas_call(
+        hand_on_kernel,
+        name="hand_on",
+        out_shape=(jax.ShapeDtypeStruct((ROWS, 256), BF16),) * 3,
+        in_specs=[VMEM] * 3,
+        out_specs=(VMEM,) * 3,
+        compiler_params=pltpu.CompilerParams(vmem_limit_bytes=LIMIT),
+    )(*results)
+
+
 def shards(queries, keys, values, attn_out, out_grad, out_weight, log_norm, block_sizes):
-    return pl.pallas_call(
+    results = pl.pallas_call(
         layer_kernel,
         name="layer",
         out_shape=(jax.ShapeDtypeStruct((ROWS, 256), BF16),) * 3,
-        in_specs=[SMEM] + [VMEM] * 7,
+        in_specs=[SMEM] + [ANY] * 5 + [VMEM] * 2,
         out_specs=(VMEM,) * 3,
         scratch_shapes=[
+            pltpu.VMEM((64, 4096), BF16),
+            pltpu.VMEM((256, 4096), BF16),
+            pltpu.VMEM((8, 64, 256), BF16),
+            pltpu.VMEM((ROWS, 256), BF16),
+            pltpu.VMEM((ROWS, 256), BF16),
             pltpu.VMEM((7, 2, UNIT, 4096), BF16),
             pltpu.VMEM((2, 8, 256, HD), BF16),
             pltpu.VMEM((2, 8, 4, 64 + SIDE, HD), BF16),
@@ -482,9 +535,10 @@
             pltpu.VMEM((8, 2, 64 + SIDE, HD), BF16),
             pltpu.VMEM((8, 2, SIDE, HD), F32),
             pltpu.VMEM((2, 256, HD), BF16),
+            pltpu.VMEM((2, 2, HD, 256), BF16),
             pltpu.VMEM((2, 256, HD), F32),
-            pltpu.VMEM((TASK_K, HD), F32),
-            pltpu.VMEM((TASK_K, HD), F32),
+            pltpu.VMEM((8, HD, 256), F32),
+            pltpu.VMEM((8, HD, 256), F32),
             pltpu.VMEM((2, 8, 256, HD), jnp.int32),
             pltpu.VMEM((8, 1, 256), jnp.int32),
             pltpu.VMEM((ROWS, HD), jnp.int32),
@@ -495,17 +549,18 @@
             pltpu.VMEM((8, 2, STRIPE, HD), BF16),
             pltpu.VMEM((4, 8, 64, 256), BF16),
             pltpu.VMEM((2, 2, ROWS, 256), BF16),
-            DMA((2, 7)), DMA((2, 7)), DMA((8,)), DMA((CHIPS,)), DMA((CHIPS,)), DMA((8,)),
+            DMA((2, 7, 2)), DMA((2, 7, 2)), DMA((8,)), DMA((CHIPS,)), DMA((CHIPS,)), DMA((8,)),
             DMA, DMA, DMA, DMA((8,)),
-            DMA((8,)), DMA, DMA, DMA, DMA((8,)), DMA, DMA,
+            DMA((8,)), DMA, DMA, DMA, DMA((8,)), DMA, DMA, DMA((5,)),
         ],
         compiler_params=pltpu.CompilerParams(
             collective_id=0, has_side_effects=True, vmem_limit_bytes=LIMIT
         ),
     )(
-        block_sizes, queries.reshape(8, 64, 256), keys, values, attn_out, out_grad, out_weight,
+        block_sizes, queries.reshape(8, 64, 256), keys, values, out_grad, out_weight, attn_out,
         log_norm.T,
     )
+    return hand_on(results)
 
 
 def solution(mesh):

time: 96.2 us -> 90.6 us (0.942)
  local copies, waits for them, and re-layouts: 5.01 us -> 0 us
    unnamed x3 -> x0, local copies, waits for them, and re-layouts: 5.01 us -> none
    pallas_call x1, Pallas kernels: 89.4 us -> 86.8 us  [shards(): pl.pallas_call(layer_kernel, name='layer', out_shape=(jax.ShapeDtypeStruc...]
    pallas_call x0 -> x1, Pallas kernels: none -> 2 us  [hand_on(): pl.pallas_call(hand_on_kernel, name='hand_on', out_shape=(jax.ShapeDtypeS...]
where the time goes in v4:
time: 90.6 us; the launch traced here: 89.5 us
  Pallas kernels  88.8 us (98%)
    pallas_call x1, Pallas kernels, shards(): pl.pallas_call(layer_kernel, name='layer', out_shape=(jax.ShapeDtypeStruc...  86.8 us
    pallas_call x1, Pallas kernels, hand_on(): pl.pallas_call(hand_on_kernel, name='hand_on', out_shape=(jax.ShapeDtypeS...  2 us

profile of v4, /device:TPU:7, one launch (start us, length us, event | category | flops | bytes accessed | tf_op | source)
XLA Modules:
  0.0 89.5 jit_solution(13765767687716434880)
XLA Ops:
  0.6 86.8 %layer.1 = (bf16[512,256]{1,0:T(8,128)(2,1)}, bf16[512,256]{1,0:T(8,128)(2,1)}, bf16[512,256]{1,0:T(8,128)(2,1)}) custom-call(s32[512]{0:T(512)} %sizes.1, bf16[8,64,256]{2,1,0:T(8,128)(2,1)} %bitcast.2, bf16[512,256]{1,0:T(8,128)(2,1)} %k_ref.1, bf16[512,256]{1,0:T(8,128)(2,1)} %v_ref.1, bf16[64,4096]{1,0:T(8,128)(2,1)} %g_hbm.1, bf16[256,4096]{1,0:T(8,128)(2,1)} %w_hbm.1, ...), custom_call_target="tpu_custom_call" | custom-call | tf_op jit(solution)/shard_map/layer/pallas_call | solution.py:518
  87.5 2.0 %hand_on.1 = (bf16[512,256]{1,0:T(8,128)(2,1)}, bf16[512,256]{1,0:T(8,128)(2,1)}, bf16[512,256]{1,0:T(8,128)(2,1)}) custom-call(bf16[512,256]{1,0:T(8,128)(2,1)} %get-tuple-element.6.refs_0_, bf16[512,256]{1,0:T(8,128)(2,1)} %get-tuple-element.7.refs_1_, bf16[512,256]{1,0:T(8,128)(2,1)} %get-tuple-element.8.refs_2_), custom_call_target="tpu_custom_call" | custom-call | tf_op jit(solution)/shard_map/hand_on/pallas_call | solution.py:507

commit v5 on v4

--- a/solution.py
+++ b/solution.py
@@ -374,28 +374,32 @@
 
     lax.fori_loop(0, 7, step, 0)
 
-    def narrow(index, carry):
+    def across(index):
+        return pltpu.make_async_remote_copy(
+            src_ref=to_sibling.at[index], dst_ref=from_sibling.at[index],
+            send_sem=sibling_send.at[index], recv_sem=sibling_recv.at[index],
+            device_id=(sibling, head), device_id_type=MESH,
+        )
+
+    def narrow(step, carry):
+        index = lax.rem(me // 2 + step, 8)
         there = pl.ds(multiple((1 - core) * STRIPE, STRIPE), STRIPE)
-        to_sibling[0, index] = (dk_sum[index, :, there] * SCALE).T.astype(BF16)
-        to_sibling[1, index] = dv_sum[index, :, there].T.astype(BF16)
+        to_sibling[index, 0] = (dk_sum[index, :, there] * SCALE).T.astype(BF16)
+        to_sibling[index, 1] = dv_sum[index, :, there].T.astype(BF16)
+        across(index).start()
         return carry
 
     lax.fori_loop(0, 8, narrow, 0)
-    across = pltpu.make_async_remote_copy(
-        src_ref=to_sibling, dst_ref=from_sibling, send_sem=sibling_send, recv_sem=sibling_recv,
-        device_id=(sibling, head), device_id_type=MESH,
-    )
-    across.start()
-    across.wait_recv()
 
     def pass_on(step, carry):
         index = lax.rem(me // 2 + step, 8)
         here = pl.ds(multiple(core * STRIPE, STRIPE), STRIPE)
+        across(index).wait_recv()
         key_part[index, 0] = (
-            (dk_sum[index, :, here] * SCALE).T + from_sibling[0, index].astype(F32)
+            (dk_sum[index, :, here] * SCALE).T + from_sibling[index, 0].astype(F32)
         ).astype(BF16)
         key_part[index, 1] = (
-            dv_sum[index, :, here].T + from_sibling[1, index].astype(F32)
+            dv_sum[index, :, here].T + from_sibling[index, 1].astype(F32)
         ).astype(BF16)
         push(
             key_part.at[index],
@@ -438,28 +442,10 @@
                 dk_out[rows, columns] = (dk * SCALE).T.astype(BF16)
                 dv_out[rows, columns] = dv.T.astype(BF16)
 
-    wait_bytes(rq, dq_recv)
-
-    def summed_queries():
-        parts = [rq[stripe].reshape(ROWS, 256).astype(F32) for stripe in range(4)]
-        return (parts[0] + parts[1]) + (parts[2] + parts[3])
-
-    @pl.when(me < SHARDS)
-    def _():
-        dq_out[...] = (summed_queries() + dq_own[...]).astype(BF16)
-
-    @pl.when(clean)
-    def _():
-        dq_out[...] = summed_queries().astype(BF16)
-        wait_bytes(rk, part_recv)
-        dk_out[...] = (rk[0, 0].astype(F32) + rk[1, 0].astype(F32)).astype(BF16)
-        dv_out[...] = (rk[0, 1].astype(F32) + rk[1, 1].astype(F32)).astype(BF16)
-
     for index in range(7):
         for direction in range(2):
             for sub in range(2):
                 ring(direction, index, sub, landed.at[index, direction]).wait_send()
-    across.wait_send()
     relay(kg, k_recv).wait_send()
 
     def settle(index, carry):
@@ -467,14 +453,6 @@
         def _():
             wait_bytes(q_ref.at[:, :, pl.ds(0, HD)], q_send.at[index])
             wait_bytes(dl.at[:, 0], d_send.at[index])
-
-        @pl.when(query_owner(index) != me)
-        def _():
-            wait_bytes(dq_part.at[:, index], dq_send.at[index])
-
-        @pl.when(SHARDS + 2 * index + core != me)
-        def _():
-            wait_bytes(key_part.at[index], part_send.at[index])
         return carry
 
     lax.fori_loop(0, 8, settle, 0)
@@ -489,6 +467,37 @@
             return carry
 
         lax.fori_loop(0, CHIPS, settle_keys, 0)
+
+    wait_bytes(rq, dq_recv)
+
+    def summed_queries():
+        parts = [rq[stripe].reshape(ROWS, 256).astype(F32) for stripe in range(4)]
+        return (parts[0] + parts[1]) + (parts[2] + parts[3])
+
+    @pl.when(me < SHARDS)
+    def _():
+        dq_out[...] = (summed_queries() + dq_own[...]).astype(BF16)
+
+    @pl.when(clean)
+    def _():
+        dq_out[...] = summed_queries().astype(BF16)
+        wait_bytes(rk, part_recv)
+        dk_out[...] = (rk[0, 0].astype(F32) + rk[1, 0].astype(F32)).astype(BF16)
+        dv_out[...] = (rk[0, 1].astype(F32) + rk[1, 1].astype(F32)).astype(BF16)
+
+    def settle_last(index, carry):
+        across(index).wait_send()
+
+        @pl.when(query_owner(index) != me)
+        def _():
+            wait_bytes(dq_part.at[:, index], dq_send.at[index])
+
+        @pl.when(SHARDS + 2 * index + core != me)
+        def _():
+            wait_bytes(key_part.at[index], part_send.at[index])
+        return carry
+
+    lax.fori_loop(0, 8, settle_last, 0)
 
 
 ANY = pl.BlockSpec(memory_space=pl.ANY)
@@ -544,14 +553,14 @@
             pltpu.VMEM((ROWS, HD), jnp.int32),
             pltpu.VMEM((ROWS, 256), F32),
             pltpu.VMEM((8, 8, 64, HD), BF16),
-            pltpu.VMEM((2, 8, STRIPE, HD), BF16),
-            pltpu.VMEM((2, 8, STRIPE, HD), BF16),
+            pltpu.VMEM((8, 2, STRIPE, HD), BF16),
+            pltpu.VMEM((8, 2, STRIPE, HD), BF16),
             pltpu.VMEM((8, 2, STRIPE, HD), BF16),
             pltpu.VMEM((4, 8, 64, 256), BF16),
             pltpu.VMEM((2, 2, ROWS, 256), BF16),
             DMA((2, 7, 2)), DMA((2, 7, 2)), DMA((8,)), DMA((CHIPS,)), DMA((CHIPS,)), DMA((8,)),
             DMA, DMA, DMA, DMA((8,)),
-            DMA((8,)), DMA, DMA, DMA, DMA((8,)), DMA, DMA, DMA((5,)),
+            DMA((8,)), DMA, DMA((8,)), DMA((8,)), DMA((8,)), DMA, DMA, DMA((5,)),
         ],
         compiler_params=pltpu.CompilerParams(
             collective_id=0, has_side_effects=True, vmem_limit_bytes=LIMIT

time: 90.6 us -> 90.1 us (level)
  no operation moved by 1% of the time
where the time goes in v5:
time: 90.1 us; the launch traced here: 88.8 us
  Pallas kernels  88.2 us (98%)
    pallas_call x1, Pallas kernels, shards(): pl.pallas_call(layer_kernel, name='layer', out_shape=(jax.ShapeDtypeStruc...  86.2 us
    pallas_call x1, Pallas kernels, hand_on(): pl.pallas_call(hand_on_kernel, name='hand_on', out_shape=(jax.ShapeDtypeS...  2 us

profile of v5, /device:TPU:7, one launch (start us, length us, event | category | flops | bytes accessed | tf_op | source)
XLA Modules:
  0.0 88.8 jit_solution(12226740686702955707)
XLA Ops:
  0.6 86.2 %layer.1 = (bf16[512,256]{1,0:T(8,128)(2,1)}, bf16[512,256]{1,0:T(8,128)(2,1)}, bf16[512,256]{1,0:T(8,128)(2,1)}) custom-call(s32[512]{0:T(512)} %sizes.1, bf16[8,64,256]{2,1,0:T(8,128)(2,1)} %bitcast.2, bf16[512,256]{1,0:T(8,128)(2,1)} %k_ref.1, bf16[512,256]{1,0:T(8,128)(2,1)} %v_ref.1, bf16[64,4096]{1,0:T(8,128)(2,1)} %g_hbm.1, bf16[256,4096]{1,0:T(8,128)(2,1)} %w_hbm.1, ...), custom_call_target="tpu_custom_call" | custom-call | tf_op jit(solution)/shard_map/layer/pallas_call | solution.py:527
  86.8 2.0 %hand_on.1 = (bf16[512,256]{1,0:T(8,128)(2,1)}, bf16[512,256]{1,0:T(8,128)(2,1)}, bf16[512,256]{1,0:T(8,128)(2,1)}) custom-call(bf16[512,256]{1,0:T(8,128)(2,1)} %get-tuple-element.6.refs_0_, bf16[512,256]{1,0:T(8,128)(2,1)} %get-tuple-element.7.refs_1_, bf16[512,256]{1,0:T(8,128)(2,1)} %get-tuple-element.8.refs_2_), custom_call_target="tpu_custom_call" | custom-call | tf_op jit(solution)/shard_map/hand_on/pallas_call | solution.py:516

commit v6 on v5

--- a/solution.py
+++ b/solution.py
@@ -300,10 +300,10 @@
             turned[slot, 0] = qg[slot, chunk].T
             turned[slot, 1] = dg[slot, chunk, :, 0:64, :].reshape(256, HD).T
         later = None
-        for number in range(9):
+        for number, wide in ((0, 1), (1, 1), (2, 1), (3, 1), (4, 2), (6, 2), (8, 1)):
             slot = 1 if number >= 4 else (number - group + 3) // 4
             pair = number - slot * (group + 1)
-            keys = pl.ds(multiple(pair * 256, 256), 256)
+            keys = pl.ds(multiple(pair * 256, 256), wide * 256)
             mask = None
             if number < 4 or number == 8:
                 own = row_block[slot, chunk]
@@ -313,8 +313,9 @@
                 qg[slot, chunk], grads, turned[slot, 0], turned[slot, 1], extras[slot],
                 kg[keys, :], vg[keys, :], mask,
             )
-            dk_sum[pair] += dk
-            dv_sum[pair] += dv
+            for step in range(wide):
+                dk_sum[pair + step] += dk[:, step * 256:(step + 1) * 256]
+                dv_sum[pair + step] += dv[:, step * 256:(step + 1) * 256]
             if number < 4:
                 dq_sum[slot] += dq
             else:
@@ -388,8 +389,6 @@
         to_sibling[index, 1] = dv_sum[index, :, there].T.astype(BF16)
         across(index).start()
         return carry
-
-    lax.fori_loop(0, 8, narrow, 0)
 
     def pass_on(step, carry):
         index = lax.rem(me // 2 + step, 8)
@@ -408,7 +407,13 @@
         )
         return carry
 
-    lax.fori_loop(0, 8, pass_on, 0)
+    def both(step, carry):
+        narrow(step + 2, carry)
+        return pass_on(step, carry)
+
+    lax.fori_loop(0, 2, narrow, 0)
+    lax.fori_loop(0, 6, both, 0)
+    lax.fori_loop(6, 8, pass_on, 0)
 
     for number in range(2, 5):
         fetches[number].wait()

time: 90.1 us -> 87.9 us (0.976)
  Pallas kernels: 88.2 us -> 85.7 us
    pallas_call x1, Pallas kernels: 86.2 us -> 83.7 us  [shards(): pl.pallas_call(layer_kernel, name='layer', out_shape=(jax.ShapeDtypeStruc...]
where the time goes in v6:
time: 87.9 us; the launch traced here: 86.4 us
  Pallas kernels  85.7 us (97%)
    pallas_call x1, Pallas kernels, shards(): pl.pallas_call(layer_kernel, name='layer', out_shape=(jax.ShapeDtypeStruc...  83.7 us
    pallas_call x1, Pallas kernels, hand_on(): pl.pallas_call(hand_on_kernel, name='hand_on', out_shape=(jax.ShapeDtypeS...  2 us

profile of v6, /device:TPU:7, one launch (start us, length us, event | category | flops | bytes accessed | tf_op | source)
XLA Modules:
  0.0 86.4 jit_solution(10583104454715153745)
XLA Ops:
  0.6 83.7 %layer.1 = (bf16[512,256]{1,0:T(8,128)(2,1)}, bf16[512,256]{1,0:T(8,128)(2,1)}, bf16[512,256]{1,0:T(8,128)(2,1)}) custom-call(s32[512]{0:T(512)} %sizes.1, bf16[8,64,256]{2,1,0:T(8,128)(2,1)} %bitcast.2, bf16[512,256]{1,0:T(8,128)(2,1)} %k_ref.1, bf16[512,256]{1,0:T(8,128)(2,1)} %v_ref.1, bf16[64,4096]{1,0:T(8,128)(2,1)} %g_hbm.1, bf16[256,4096]{1,0:T(8,128)(2,1)} %w_hbm.1, ...), custom_call_target="tpu_custom_call" | custom-call | tf_op jit(solution)/shard_map/layer/pallas_call | solution.py:532
  84.4 2.0 %hand_on.1 = (bf16[512,256]{1,0:T(8,128)(2,1)}, bf16[512,256]{1,0:T(8,128)(2,1)}, bf16[512,256]{1,0:T(8,128)(2,1)}) custom-call(bf16[512,256]{1,0:T(8,128)(2,1)} %get-tuple-element.6.refs_0_, bf16[512,256]{1,0:T(8,128)(2,1)} %get-tuple-element.7.refs_1_, bf16[512,256]{1,0:T(8,128)(2,1)} %get-tuple-element.8.refs_2_), custom_call_target="tpu_custom_call" | custom-call | tf_op jit(solution)/shard_map/hand_on/pallas_call | solution.py:521

commit v7 on v6

--- a/solution.py
+++ b/solution.py
@@ -300,7 +300,7 @@
             turned[slot, 0] = qg[slot, chunk].T
             turned[slot, 1] = dg[slot, chunk, :, 0:64, :].reshape(256, HD).T
         later = None
-        for number, wide in ((0, 1), (1, 1), (2, 1), (3, 1), (4, 2), (6, 2), (8, 1)):
+        for number, wide in ((0, 1), (1, 1), (2, 1), (3, 1), (4, 4), (8, 1)):
             slot = 1 if number >= 4 else (number - group + 3) // 4
             pair = number - slot * (group + 1)
             keys = pl.ds(multiple(pair * 256, 256), wide * 256)

time: 87.9 us -> 87 us (0.990)
  no operation moved by 1% of the time
where the time goes in v7:
time: 87 us; the launch traced here: 85.9 us
  Pallas kernels  85.2 us (98%)
    pallas_call x1, Pallas kernels, shards(): pl.pallas_call(layer_kernel, name='layer', out_shape=(jax.ShapeDtypeStruc...  83.2 us
    pallas_call x1, Pallas kernels, hand_on(): pl.pallas_call(hand_on_kernel, name='hand_on', out_shape=(jax.ShapeDtypeS...  2 us

profile of v7, /device:TPU:7, one launch (start us, length us, event | category | flops | bytes accessed | tf_op | source)
XLA Modules:
  0.0 85.9 jit_solution(604474040024393769)
XLA Ops:
  0.6 83.2 %layer.1 = (bf16[512,256]{1,0:T(8,128)(2,1)}, bf16[512,256]{1,0:T(8,128)(2,1)}, bf16[512,256]{1,0:T(8,128)(2,1)}) custom-call(s32[512]{0:T(512)} %sizes.1, bf16[8,64,256]{2,1,0:T(8,128)(2,1)} %bitcast.2, bf16[512,256]{1,0:T(8,128)(2,1)} %k_ref.1, bf16[512,256]{1,0:T(8,128)(2,1)} %v_ref.1, bf16[64,4096]{1,0:T(8,128)(2,1)} %g_hbm.1, bf16[256,4096]{1,0:T(8,128)(2,1)} %w_hbm.1, ...), custom_call_target="tpu_custom_call" | custom-call | tf_op jit(solution)/shard_map/layer/pallas_call | solution.py:532
  83.9 2.0 %hand_on.1 = (bf16[512,256]{1,0:T(8,128)(2,1)}, bf16[512,256]{1,0:T(8,128)(2,1)}, bf16[512,256]{1,0:T(8,128)(2,1)}) custom-call(bf16[512,256]{1,0:T(8,128)(2,1)} %get-tuple-element.6.refs_0_, bf16[512,256]{1,0:T(8,128)(2,1)} %get-tuple-element.7.refs_1_, bf16[512,256]{1,0:T(8,128)(2,1)} %get-tuple-element.8.refs_2_), custom_call_target="tpu_custom_call" | custom-call | tf_op jit(solution)/shard_map/hand_on/pallas_call | solution.py:521
